TPU v7x, 32 devices: a whole 2x2x4 slice. The times are simulated.
32 devices in a mesh: dom: 8 (over y, x, core), rep: 4 (over z).
Axes of the slice: x: 2, y: 2, z: 4, core: 2. Of those that a mesh axis runs over, the one named last changes fastest.
Arguments:
- codes: bfloat16 [16384, 256], P('dom'), may hold values from -1.5 to 1.5
- scales: bfloat16 [16384], P('dom'), may hold values from 0.5 to 2
- accum: float32 [16384], P('dom'), may hold values from 0.01 to 1
- relations: bfloat16 [64, 256], replicated, may hold values from -5 to 5
- matching: int32 [8], P('dom'), may hold values from 0 to 7, as said below
- edges: int32 [3, 131072], P(None, ('dom', 'rep')), may hold values from 0 to 2047, as said below
- counts: int32 [32], P(('dom', 'rep')), may hold values from 1 to 4096, 65536 in all
- negatives: int32 [256, 1024], P(('dom', 'rep')), may hold values from 0 to 2047
Outputs:
- new_codes: bfloat16 [16384, 256], P('dom')
- new_accum: float32 [16384], P(('dom', 'rep'))
Inputs may be any that keep to these rules, and one draw needn't show every extreme that they name: matching[b] = b XOR m for one m from 1 to 7 shared by all buckets, so partitions pair up. `edges`: rows 0 and 2 hold row ids below 2048, row 1 relation ids below 64.
All inputs are finite; a program needn't handle non-finite values. No bound on the sum of `counts` on one device may be relied on, other than what follows from the above.
Results may differ from a plain program's by a relative error of at most 0.0075.
Values may be sent and summed in bfloat16 or wider, within the bound.
No kernel may reach another device: no remote copies, remote signals or barrier semaphores. Data moves between devices by JAX's collectives and lax.ppermute only.
A program may use at most 64 MiB of HBM per device.

v0:
```python
import jax
import jax.numpy as jnp
from jax import lax
from jax.sharding import PartitionSpec as P

GROUP = 512


LEARN_RATE = 0.1
ROOT_EPSILON = 1e-08


def from_partner(block, axis, apart):
    count = lax.axis_size(axis)
    route = []
    for low in range(count):
        high = low | 1 << apart
        if high != low and high < count:
            route += [(low, high), (high, low)]
    return lax.ppermute(block, axis, route)


def group_terms(src_block, dst_block, relation_rows, src_ids, dst_ids, live_mask, negative_ids):
    source_rows = jnp.take(src_block, src_ids, axis=0).astype(jnp.float32)
    target_rows = jnp.take(dst_block, dst_ids, axis=0)
    negative_rows = jnp.take(dst_block, negative_ids, axis=0)
    query = (source_rows * relation_rows).astype(jnp.bfloat16)
    positive = jnp.sum(query.astype(jnp.float32) * target_rows.astype(jnp.float32), axis=1)
    scores = jnp.dot(query, negative_rows.T, preferred_element_type=jnp.float32)
    weight = live_mask.astype(jnp.float32)
    pos_coef = -weight * jax.nn.sigmoid(-positive)
    neg_coef = (weight[:, None] * jax.nn.sigmoid(scores) / negative_rows.shape[0]).astype(
        jnp.bfloat16
    )
    query_grad = pos_coef[:, None] * target_rows.astype(jnp.float32) + jnp.dot(
        neg_coef, negative_rows, preferred_element_type=jnp.float32
    )
    source_grad = query_grad * relation_rows
    target_grad = pos_coef[:, None] * query.astype(jnp.float32)
    negative_grad = lax.dot_general(
        neg_coef, query, (((0,), (0,)), ((), ())), preferred_element_type=jnp.float32
    )
    return (source_grad, target_grad, negative_grad)


def partner_bit(partner_bits, bit_index):
    return jnp.bitwise_and(jnp.right_shift(partner_bits, bit_index), 1) == 1


def body(codes, scales, accum, relations, matching, edges, counts, negatives):
    dom_bits = lax.axis_size("dom").bit_length() - 1
    rep_count = lax.axis_size("rep")
    partner_bits = jnp.bitwise_xor(matching[0], lax.axis_index("dom"))
    values = codes.astype(jnp.float32) * scales.astype(jnp.float32)[:, None]
    src_block = values.astype(jnp.bfloat16)
    dst_block = src_block
    for bit_index in range(dom_bits):
        arrived = from_partner(dst_block, "dom", bit_index)
        dst_block = jnp.where(partner_bit(partner_bits, bit_index), arrived, dst_block)
    part_rows = codes.shape[0]
    slots = edges.shape[1]
    group_len = GROUP
    group_total = slots // group_len
    live_mask = (jnp.arange(slots, dtype=jnp.int32) < counts[0]).astype(jnp.int32)
    edge_pack = jnp.concatenate([edges, live_mask[None, :]], axis=0).reshape(
        4, group_total, group_len
    )
    rel_count = relations.shape[0]

    def group_step(position, carry):
        block_ids = lax.dynamic_index_in_dim(edge_pack, position, 1, keepdims=False)
        block_negs = lax.dynamic_index_in_dim(negatives, position, 0, keepdims=False)

        def score_group(grads_in):
            one_hot = jax.nn.one_hot(block_ids[1], rel_count, dtype=jnp.bfloat16)
            relation_rows = jnp.dot(one_hot, relations, preferred_element_type=jnp.float32)
            source_grad, target_grad, negative_grad = group_terms(
                src_block,
                dst_block,
                relation_rows,
                block_ids[0],
                block_ids[2],
                block_ids[3],
                block_negs,
            )
            first = grads_in[0].at[block_ids[0]].add(source_grad)
            second = grads_in[1].at[block_ids[2]].add(target_grad).at[block_negs].add(negative_grad)
            return (first, second)

        return lax.cond(jnp.any(block_ids[3] > 0), score_group, lambda grads_in: grads_in, carry)

    empty = jnp.zeros((part_rows, values.shape[1]), jnp.float32)
    src_grad, dst_grad = lax.fori_loop(0, group_total, group_step, (empty, empty))
    share_rows = part_rows // rep_count
    first_row = lax.axis_index("rep") * share_rows
    returned = dst_grad
    for bit_index in range(dom_bits):
        arrived = from_partner(returned.astype(jnp.bfloat16), "dom", bit_index).astype(
            returned.dtype
        )
        returned = jnp.where(partner_bit(partner_bits, bit_index), arrived, returned)
    summed = lax.psum(src_grad + returned, "rep")
    state = accum + jnp.mean(summed * summed, axis=1)
    updated = values - LEARN_RATE * summed / (jnp.sqrt(state)[:, None] + ROOT_EPSILON)
    new_codes = (updated / scales.astype(jnp.float32)[:, None]).astype(jnp.bfloat16)
    new_accum = lax.dynamic_slice_in_dim(state, first_row, share_rows, 0)
    return (new_codes, new_accum)


def solution(mesh):
    placed = (
        P("dom", None),
        P("dom"),
        P("dom"),
        P(),
        P("dom"),
        P(None, ("dom", "rep")),
        P(("dom", "rep")),
        P(("dom", "rep"), None),
    )
    return jax.shard_map(
        body,
        mesh=mesh,
        in_specs=placed,
        out_specs=(P("dom", None), P(("dom", "rep"))),
        check_vma=False,
    )
```

profile of v0, /device:TPU:0, one launch (start us, length us, event | category | flops | bytes accessed | tf_op | source)
XLA Modules:
  0.0 595.5 jit_solution(6844182797904183809)
XLA Ops:
  13.2 2.9 collective-permute-start.1
  16.1 23.6 %collective-permute-done.1 = bf16[2048,256]{1,0:T(8,128)(2,1)} collective-permute-done((bf16[2048,256]{1,0:T(8,128)(2,1)S(1)}, bf16[2048,256]{1,0:T(8,128)(2,1)}, u32[]{:S(2)}, u32[]{:S(2)}) %collective-permute-start.1) | collective-permute-done | bytes 1048608 | tf_op jit(solution)/shard_map/ppermute | solution.py:20
  42.4 22.3 %collective-permute-done.2 = bf16[2048,256]{1,0:T(8,128)(2,1)} collective-permute-done((bf16[2048,256]{1,0:T(8,128)(2,1)S(1)}, bf16[2048,256]{1,0:T(8,128)(2,1)}, u32[]{:S(2)}, u32[]{:S(2)}) %collective-permute-start.2) | collective-permute-done | bytes 1048608 | tf_op jit(solution)/shard_map/ppermute | solution.py:20
  67.6 192.8 %while.15 = (s32[]{:T(128)}, f32[2048,256]{1,0:T(8,128)}, f32[2048,256]{1,0:T(8,128)S(1)}, s32[4,8,512]{2,1,0:T(8,128)S(1)}, bf16[2048,256]{1,0:T(8,128)(2,1)}, ...) while((s32[]{:T(128)}, f32[2048,256]{1,0:T(8,128)}, ...), condition=%wide.region_8.10_spmd, body=%wide.region_0.9_spmd.sunk | while | flops 828435456 | bytes 30310256 | solution.py:93
  69.1 45.3 %conditional.2 = ((f32[2048,256]{1,0:T(8,128)}, f32[2048,256]{1,0:T(8,128)S(1)})) conditional(s32[]{:T(128)} %convert_element_type.145, (f32[2048,256]{1,0:T(8,128)}, f32[2048,256]{1,0:T(8,128)S(1)}) %tuple.53, (s32[4,1,512]{2,1,0:T(1,128)S(1)}, bf16[2048,256]{1,0:T(8,128)(2,1)}, bf16[64,256]{1,0:T(8,128)(2,1)S(1)}, bf16[2048,256]{1,0:T(8,128)(2,1)S(1)}, ...), branch_computations={%region_2.2_spmd, %region_3.8_spmd} | conditional | flops 828434432 | bytes 30291596 | solution.py:90
  72.0 2.9 gather_fusion.1
  78.7 5.0 gather_fusion
  90.5 6.4 %scatter_fusion = f32[2048,256]{1,0:T(8,128)} fusion(f32[2048,256]{1,0:T(8,128)} %get-tuple-element.174, s32[512]{0:T(512)S(1)} %bitcast.35, f32[512,256]{1,0:T(8,128)} %copy.16), kind=kCustom, calls=%fused_computation.3 | custom fusion | flops 131072 | bytes 1574912 | tf_op jit(solution)/shard_map/while/body/eval_jaxpr/cond/branch_1_fun/scatter-add | solution.py:86
  99.8 4.6 scatter_fusion.1
  107.1 7.3 %scatter_fusion.2 = f32[2048,256]{1,0:T(8,128)S(1)} fusion(f32[2048,256]{1,0:T(8,128)S(1)} %scatter_fusion.1, s32[1024]{0:T(1024)S(1)} %bitcast.28, f32[1024,256]{1,0:T(8,128)} %fusion.10), kind=kCustom, calls=%fused_computation.5 | custom fusion | flops 262144 | bytes 3149824 | tf_op jit(solution)/shard_map/while/body/eval_jaxpr/cond/branch_1_fun/scatter-add | solution.py:87
  115.8 45.3 %conditional.2 = ((f32[2048,256]{1,0:T(8,128)}, f32[2048,256]{1,0:T(8,128)S(1)})) conditional(s32[]{:T(128)} %convert_element_type.145, (f32[2048,256]{1,0:T(8,128)}, f32[2048,256]{1,0:T(8,128)S(1)}) %tuple.53, (s32[4,1,512]{2,1,0:T(1,128)S(1)}, bf16[2048,256]{1,0:T(8,128)(2,1)}, bf16[64,256]{1,0:T(8,128)(2,1)S(1)}, bf16[2048,256]{1,0:T(8,128)(2,1)S(1)}, ...), branch_computations={%region_2.2_spmd, %region_3.8_spmd} | conditional | flops 828434432 | bytes 30291596 | solution.py:90
  118.7 2.9 gather_fusion.1
  125.5 5.0 gather_fusion
  137.2 6.4 %scatter_fusion = f32[2048,256]{1,0:T(8,128)} fusion(f32[2048,256]{1,0:T(8,128)} %get-tuple-element.174, s32[512]{0:T(512)S(1)} %bitcast.35, f32[512,256]{1,0:T(8,128)} %copy.16), kind=kCustom, calls=%fused_computation.3 | custom fusion | flops 131072 | bytes 1574912 | tf_op jit(solution)/shard_map/while/body/eval_jaxpr/cond/branch_1_fun/scatter-add | solution.py:86
  146.5 4.6 scatter_fusion.1
  153.8 7.3 %scatter_fusion.2 = f32[2048,256]{1,0:T(8,128)S(1)} fusion(f32[2048,256]{1,0:T(8,128)S(1)} %scatter_fusion.1, s32[1024]{0:T(1024)S(1)} %bitcast.28, f32[1024,256]{1,0:T(8,128)} %fusion.10), kind=kCustom, calls=%fused_computation.5 | custom fusion | flops 262144 | bytes 3149824 | tf_op jit(solution)/shard_map/while/body/eval_jaxpr/cond/branch_1_fun/scatter-add | solution.py:87
  162.5 45.3 %conditional.2 = ((f32[2048,256]{1,0:T(8,128)}, f32[2048,256]{1,0:T(8,128)S(1)})) conditional(s32[]{:T(128)} %convert_element_type.145, (f32[2048,256]{1,0:T(8,128)}, f32[2048,256]{1,0:T(8,128)S(1)}) %tuple.53, (s32[4,1,512]{2,1,0:T(1,128)S(1)}, bf16[2048,256]{1,0:T(8,128)(2,1)}, bf16[64,256]{1,0:T(8,128)(2,1)S(1)}, bf16[2048,256]{1,0:T(8,128)(2,1)S(1)}, ...), branch_computations={%region_2.2_spmd, %region_3.8_spmd} | conditional | flops 828434432 | bytes 30291596 | solution.py:90
  165.5 2.9 gather_fusion.1
  172.2 5.0 gather_fusion
  184.0 6.4 %scatter_fusion = f32[2048,256]{1,0:T(8,128)} fusion(f32[2048,256]{1,0:T(8,128)} %get-tuple-element.174, s32[512]{0:T(512)S(1)} %bitcast.35, f32[512,256]{1,0:T(8,128)} %copy.16), kind=kCustom, calls=%fused_computation.3 | custom fusion | flops 131072 | bytes 1574912 | tf_op jit(solution)/shard_map/while/body/eval_jaxpr/cond/branch_1_fun/scatter-add | solution.py:86
  193.3 4.6 scatter_fusion.1
  200.5 7.3 %scatter_fusion.2 = f32[2048,256]{1,0:T(8,128)S(1)} fusion(f32[2048,256]{1,0:T(8,128)S(1)} %scatter_fusion.1, s32[1024]{0:T(1024)S(1)} %bitcast.28, f32[1024,256]{1,0:T(8,128)} %fusion.10), kind=kCustom, calls=%fused_computation.5 | custom fusion | flops 262144 | bytes 3149824 | tf_op jit(solution)/shard_map/while/body/eval_jaxpr/cond/branch_1_fun/scatter-add | solution.py:87
  209.3 45.3 %conditional.2 = ((f32[2048,256]{1,0:T(8,128)}, f32[2048,256]{1,0:T(8,128)S(1)})) conditional(s32[]{:T(128)} %convert_element_type.145, (f32[2048,256]{1,0:T(8,128)}, f32[2048,256]{1,0:T(8,128)S(1)}) %tuple.53, (s32[4,1,512]{2,1,0:T(1,128)S(1)}, bf16[2048,256]{1,0:T(8,128)(2,1)}, bf16[64,256]{1,0:T(8,128)(2,1)S(1)}, bf16[2048,256]{1,0:T(8,128)(2,1)S(1)}, ...), branch_computations={%region_2.2_spmd, %region_3.8_spmd} | conditional | flops 828434432 | bytes 30291596 | solution.py:90
  212.2 2.9 gather_fusion.1
  219.0 5.0 gather_fusion
  230.7 6.4 %scatter_fusion = f32[2048,256]{1,0:T(8,128)} fusion(f32[2048,256]{1,0:T(8,128)} %get-tuple-element.174, s32[512]{0:T(512)S(1)} %bitcast.35, f32[512,256]{1,0:T(8,128)} %copy.16), kind=kCustom, calls=%fused_computation.3 | custom fusion | flops 131072 | bytes 1574912 | tf_op jit(solution)/shard_map/while/body/eval_jaxpr/cond/branch_1_fun/scatter-add | solution.py:86
  240.0 4.6 scatter_fusion.1
  247.3 7.3 %scatter_fusion.2 = f32[2048,256]{1,0:T(8,128)S(1)} fusion(f32[2048,256]{1,0:T(8,128)S(1)} %scatter_fusion.1, s32[1024]{0:T(1024)S(1)} %bitcast.28, f32[1024,256]{1,0:T(8,128)} %fusion.10), kind=kCustom, calls=%fused_computation.5 | custom fusion | flops 262144 | bytes 3149824 | tf_op jit(solution)/shard_map/while/body/eval_jaxpr/cond/branch_1_fun/scatter-add | solution.py:87
  263.6 25.2 %collective-permute-done.4 = bf16[2048,256]{1,0:T(8,128)(2,1)S(1)} collective-permute-done((bf16[2048,256]{1,0:T(8,128)(2,1)S(1)}, bf16[2048,256]{1,0:T(8,128)(2,1)S(1)}, u32[]{:S(2)}, u32[]{:S(2)}) %collective-permute-start.4) | collective-permute-done | bytes 1048608 | tf_op jit(solution)/shard_map/ppermute | solution.py:20
  289.1 182.7 %collective-permute-start.5 = (bf16[2048,256]{1,0:T(8,128)(2,1)S(1)}, bf16[2048,256]{1,0:T(8,128)(2,1)S(1)}, u32[]{:S(2)}, u32[]{:S(2)}) collective-permute-start(bf16[2048,256]{1,0:T(8,128)(2,1)S(1)} %fusion.8), channel_id=1, source_target_pairs={{0,16},{16,0},{4,20},{20,4},{8,24},{24,8},{12,28},{28,12},{1,17},{... | collective-permute-start | bytes 3145736 | tf_op jit(solution)/shard_map/ppermute | solution.py:20
  471.7 22.6 %collective-permute-done.5 = bf16[2048,256]{1,0:T(8,128)(2,1)S(1)} collective-permute-done((bf16[2048,256]{1,0:T(8,128)(2,1)S(1)}, bf16[2048,256]{1,0:T(8,128)(2,1)S(1)}, u32[]{:S(2)}, u32[]{:S(2)}) %collective-permute-start.5) | collective-permute-done | bytes 1048608 | tf_op jit(solution)/shard_map/ppermute | solution.py:20
  496.2 88.1 %all-reduce.2.cloned.1.call-done = f32[2048,256]{1,0:T(8,128)} async-done(((f32[2048,256]{1,0:T(8,128)}), f32[2048,256]{1,0:T(8,128)}) %all-reduce.2.cloned.1.call-update) | async-done | bytes 2097168 | tf_op jit(solution)/shard_map/psum | solution.py:102
  (178 shorter events, 101.5 us)
Async XLA Ops:
  7.2 5.3 copy-start.6
  7.2 577.2 %all-reduce.2.cloned.1.call-start = ((), (), s32[]{:S(2)}) async-start(), calls=%async_computation | async-start | bytes 4194304 | tf_op jit(solution)/shard_map/psum | solution.py:102
  9.6 30.2 %copy-start.1 = (bf16[2048,256]{1,0:T(8,128)(2,1)}, bf16[2048,256]{1,0:T(8,128)(2,1)S(1)}, u32[]{:S(2)}) copy-start(bf16[2048,256]{1,0:T(8,128)(2,1)S(1)} %fusion.6) | copy-start | bytes 3145732
  9.6 2.9 collective-permute-start
  13.2 29.1 %copy-start.10 = (s32[3,4096]{1,0:T(4,128)S(1)}, s32[3,4096]{1,0:T(4,128)}, u32[]{:S(2)}) copy-start(s32[3,4096]{1,0:T(4,128)} %param.19) | copy-start | bytes 147460
  13.2 26.5 %collective-permute-start.1 = (bf16[2048,256]{1,0:T(8,128)(2,1)S(1)}, bf16[2048,256]{1,0:T(8,128)(2,1)}, u32[]{:S(2)}, u32[]{:S(2)}) collective-permute-start(bf16[2048,256]{1,0:T(8,128)(2,1)S(1)} %broadcast_select_fusion.4), channel_id=1, source_target_pairs={{0,8},{8,0},{4,12},{12,4},{16,24},{24,16},{20,28},{28,20},{1,9},{9... | collective-permute-start | bytes 3145736 | tf_op jit(solution)/shard_map/ppermute | solution.py:20
  39.8 24.9 %collective-permute-start.2 = (bf16[2048,256]{1,0:T(8,128)(2,1)S(1)}, bf16[2048,256]{1,0:T(8,128)(2,1)}, u32[]{:S(2)}, u32[]{:S(2)}) collective-permute-start(bf16[2048,256]{1,0:T(8,128)(2,1)S(1)} %broadcast_select_fusion.5), channel_id=1, source_target_pairs={{0,16},{16,0},{4,20},{20,4},{8,24},{24,8},{12,28},{28,12},{1,17},{... | collective-permute-start | bytes 3145736 | tf_op jit(solution)/shard_map/ppermute | solution.py:20
  66.0 1.6 copy-start.9
  83.7 3.1 copy-start.3
  83.7 3.1 copy-start.4
  83.7 3.1 copy-start.5
  85.8 1.0 copy-start.2
  130.5 3.1 copy-start.3
  130.5 3.1 copy-start.4
  130.5 3.1 copy-start.5
  132.5 1.0 copy-start.2
  177.2 3.1 copy-start.3
  177.2 3.1 copy-start.4
  177.2 3.1 copy-start.5
  179.3 1.0 copy-start.2
  223.9 3.1 copy-start.3
  223.9 3.1 copy-start.4
  224.0 3.1 copy-start.5
  226.0 1.0 copy-start.2
  260.5 2.7 collective-permute-start.3
  263.5 230.9 %copy-start = (f32[2048,256]{1,0:T(8,128)S(1)}, f32[2048,256]{1,0:T(8,128)}, u32[]{:S(2)}) copy-start(f32[2048,256]{1,0:T(8,128)} %get-tuple-element.197) | copy-start | bytes 6291460
  263.5 25.3 %collective-permute-start.4 = (bf16[2048,256]{1,0:T(8,128)(2,1)S(1)}, bf16[2048,256]{1,0:T(8,128)(2,1)S(1)}, u32[]{:S(2)}, u32[]{:S(2)}) collective-permute-start(bf16[2048,256]{1,0:T(8,128)(2,1)S(1)} %fusion.7), channel_id=1, source_target_pairs={{0,8},{8,0},{4,12},{12,4},{16,24},{24,16},{20,28},{28,20},{1,9},{9... | collective-permute-start | bytes 3145736 | tf_op jit(solution)/shard_map/ppermute | solution.py:20
  289.1 205.3 %collective-permute-start.5 = (bf16[2048,256]{1,0:T(8,128)(2,1)S(1)}, bf16[2048,256]{1,0:T(8,128)(2,1)S(1)}, u32[]{:S(2)}, u32[]{:S(2)}) collective-permute-start(bf16[2048,256]{1,0:T(8,128)(2,1)S(1)} %fusion.8), channel_id=1, source_target_pairs={{0,16},{16,0},{4,20},{20,4},{8,24},{24,8},{12,28},{28,12},{1,17},{... | collective-permute-start | bytes 3145736 | tf_op jit(solution)/shard_map/ppermute | solution.py:20
  496.2 90.3 %copy-start.11 = (f32[2048]{0:T(1024)S(1)}, f32[2048]{0:T(1024)}, u32[]{:S(2)}) copy-start(f32[2048]{0:T(1024)} %param.16) | copy-start | bytes 24580
  496.2 90.9 %copy-start.7 = (bf16[2048,256]{1,0:T(8,128)(2,1)S(1)}, bf16[2048,256]{1,0:T(8,128)(2,1)}, u32[]{:S(2)}) copy-start(bf16[2048,256]{1,0:T(8,128)(2,1)} %param.14) | copy-start | bytes 3145732
  584.3 2.8 copy-start.8
Sparse Core Ops, SparseCore 0:
  496.3 87.9 all-reduce.1
where the time goes:
time: 599 us; the launch traced here: 595 us
  starting transfers between devices  188 us (31%)
  waiting for transfers between devices  186 us (31%)
  other arithmetic  96 us (16%)
  local copies, waits for them, and re-layouts  68.9 us (12%)
  matrix products  34.3 us (6%)
  between operations  15.5 us (3%)
  loops' own time  6.4 us (1%)
    ppermute x6, starting transfers between devices, from_partner(): return lax.ppermute(block, axis, route)  188 us
    ppermute x6, waiting for transfers between devices, from_partner(): return lax.ppermute(block, axis, route)  98.1 us
    psum x1, waiting for transfers between devices, body(): summed = lax.psum(src_grad + returned, 'rep')  88.1 us
    scatter-add x8, other arithmetic, score_group(): grads_in[1].at[block_ids[2]].add(target_grad).at[block_negs]  47.5 us
    scatter-add x4, other arithmetic, score_group(): first = grads_in[0].at[block_ids[0]].add(source_grad)  25.6 us
    gather x4, local copies, waits for them, and re-layouts, group_terms(): negative_rows = jnp.take(dst_block, negative_ids, axis=0)  19.9 us
    gather x8, local copies, waits for them, and re-layouts, group_terms(): source_rows = jnp.take(src_block, src_ids, axis=0).astype(jnp.float32)  15.1 us
  transfers between devices with their start and end apart: 7, of which 7 were waited for; matrix products, arithmetic and copies ran while one was open for 0% of the time, Pallas kernels for 0%

commit v1 on v0

v1 whole, which is shorter than its diff:
```python
import functools

import jax
import jax.numpy as jnp
from jax import lax
from jax.experimental import pallas as pl
from jax.experimental.pallas import tpu as pltpu
from jax.sharding import PartitionSpec as P

GROUP = 512
LOW = 128
TILE = 512
NARROW = 256
HELD = 10
LAST_KEY = 2**31 - 1
LEARN_RATE = 0.1
ROOT_EPSILON = 1e-08
VMEM_LIMIT = 24 * 1024 * 1024


def swap_beside(apart, block, beside, *args):
    count = lax.axis_size("dom")

    def route(bits):
        return [(at, at ^ bits) for at in range(count)]

    if count <= 8:

        def branch(bits):
            return lambda block, *args: (lax.ppermute(block, "dom", route(bits)),) + beside(*args)

        return lax.switch(apart - 1, [branch(bits) for bits in range(1, count)], block, *args)
    for bit in range(count.bit_length() - 1):
        here = jnp.bitwise_and(jnp.right_shift(apart, bit), 1) == 1
        block = lax.cond(here, lambda b: lax.ppermute(b, "dom", route(1 << bit)), lambda b: b, block)
    return (block,) + beside(*args)


def ring_order(count):
    return list(range(0, count, 2)) + list(range(1, count, 2))[::-1]


def one_hot(rows, ids, one=1):
    step = min(rows, 256)
    spots = lax.broadcasted_iota(jnp.int32, (step, ids.shape[1]), 0).astype(jnp.bfloat16)
    low = (ids & (step - 1)).astype(jnp.float32)
    parts = []
    for first in range(0, rows, step):
        inside = (ids >= first) & (ids < first + step)
        key = jnp.where(inside, low, -1.0).astype(jnp.bfloat16)
        parts.append(jnp.where(spots == key, jnp.bfloat16(one), jnp.bfloat16(0)))
    return jnp.concatenate(parts, axis=0) if len(parts) > 1 else parts[0]


def nt_dot(a, b):
    return lax.dot_general(a, b, (((1,), (1,)), ((), ())), preferred_element_type=jnp.float32)


def nn_dot(a, b):
    return jnp.dot(a, b, preferred_element_type=jnp.float32)


def unpack(words):
    return jnp.concatenate([words & 0xFFFF, words >> 16], axis=0)


def bits_for(count):
    return (count - 1).bit_length()


class Packing:
    def __init__(self, part_rows, share, relations, blocks):
        self.half = part_rows // 2
        self.relation_at = bits_for(blocks)
        self.target_at = self.relation_at + bits_for(relations)
        self.source_at = self.target_at + bits_for(share + 1)
        assert self.source_at + bits_for(part_rows) <= 32

    def pack(self, source, target, relation, block):
        return (
            ((source - self.half) << self.source_at)
            + (target << self.target_at)
            + (relation << self.relation_at)
            + block
        )

    def bound(self, row):
        return (row - self.half) << self.source_at

    def source(self, word):
        return (word >> self.source_at) + self.half

    def target(self, word):
        return (word >> self.target_at) & ((1 << (self.source_at - self.target_at)) - 1)

    def relation(self, word):
        return (word >> self.relation_at) & ((1 << (self.target_at - self.relation_at)) - 1)

    def is_empty(self, word):
        return self.target(word) == (1 << (self.source_at - self.target_at)) - 1

    def block(self, word):
        return word & ((1 << self.relation_at) - 1)


def sort_columns(parts):
    count = len(parts)
    list_bits = bits_for(count)
    column = count * 8
    spread = max(1, TILE // column)
    low_lane_bits = bits_for(spread)
    lane_bits = [7 - low_lane_bits + k for k in range(low_lane_bits)] + list(range(7 - low_lane_bits))
    places = [("list", k) for k in range(list_bits)] + [("row", k) for k in range(3)] + [("lane", k) for k in lane_bits]
    row = lax.broadcasted_iota(jnp.int32, (8, 128), 0)
    lane = lax.broadcasted_iota(jnp.int32, (8, 128), 1)
    unset = {
        place: ((row if place[0] == "row" else lane) & (1 << place[1])) == 0
        for place in places
        if place[0] != "list"
    }
    total = len(places)

    def is_unset(index, position):
        if position == total:
            return True
        kind, bit = places[position]
        return index & (1 << bit) == 0 if kind == "list" else unset[(kind, bit)]

    def choose(mask, yes, no):
        if mask is True or mask is False:
            return yes if mask else no
        return jnp.where(mask, yes, no)

    for size in range(1, total + 1):
        for position in range(size - 1, -1, -1):
            kind, bit = places[position]
            if kind == "list":
                done = list(parts)
                for low in range(count):
                    high = low | 1 << bit
                    if high == low:
                        continue
                    up = is_unset(low, size)
                    small, large = jnp.minimum(parts[low], parts[high]), jnp.maximum(parts[low], parts[high])
                    done[low], done[high] = choose(up, small, large), choose(up, large, small)
                parts = done
                continue
            axis, extent = (0, 8) if kind == "row" else (1, 128)
            apart = 1 << bit
            first = unset[(kind, bit)]
            done = []
            for index, part in enumerate(parts):
                other = pltpu.roll(part, apart, axis)
                if 2 * apart != extent:
                    other = jnp.where(first, pltpu.roll(part, extent - apart, axis), other)
                small, large = jnp.minimum(part, other), jnp.maximum(part, other)
                up = is_unset(index, size)
                if up is True:
                    keep_small = first
                elif up is False:
                    keep_small = jnp.logical_not(first)
                else:
                    keep_small = jnp.logical_not(jnp.logical_xor(first, up))
                done.append(jnp.where(keep_small, small, large))
            parts = done
    return parts


def pick(table, place):
    out = jnp.int32(table[0])
    for at, entry in enumerate(table[1:], 1):
        out = jnp.where(place == at, jnp.int32(entry), out)
    return out


def open_kernel(tiles, share, place_ref, codes_hbm, scales_hbm, relations_hbm, edges_hbm, negatives_hbm, counts_hbm, *refs):
    reps = len(refs) - 11
    outs, refs = refs[:reps], refs[reps:]
    own_t_ref, values_t_ref, rel_t_ref, codes_ref, scales_ref, relations_ref, edges_ref, negatives_ref, counts_ref, counted, sems = refs
    place = place_ref[0]
    first = pl.multiple_of(place * share, 128)
    pairs = [
        (negatives_hbm, negatives_ref),
        (counts_hbm, counts_ref),
        (edges_hbm, edges_ref),
        (codes_hbm.at[pl.ds(first, share), :], codes_ref),
        (scales_hbm, scales_ref),
        (relations_hbm, relations_ref),
    ]
    copies = [pltpu.make_async_copy(source, target, sems.at[k]) for k, (source, target) in enumerate(pairs)]
    for copy in copies:
        copy.start()
    lanes = counted.shape[0]
    copies[0].wait()
    for block in range(tiles):
        negative = negatives_ref[block : block + 1, :]
        near = one_hot(LOW, negative & (LOW - 1))
        far = one_hot(lanes, negative >> (LOW.bit_length() - 1))
        held = nt_dot(far, near)
        for k in range(lanes):
            counted[k, block : block + 1, :] = held[k : k + 1, :]
    copies[1].wait()
    copies[2].wait()
    for apart, ids_ref in enumerate(outs):
        for tile in range(tiles):
            span = slice(tile * GROUP, (tile + 1) * GROUP)
            ids_ref[tile : tile + 1, :] = edges_ref[0:1, span] | (edges_ref[2:3, span] << 16)
        for tile in range(tiles // 2):
            near = edges_ref[1:2, tile * GROUP : (tile + 1) * GROUP]
            far = edges_ref[1:2, (tiles // 2 + tile) * GROUP : (tiles // 2 + tile + 1) * GROUP]
            ids_ref[tiles + tile : tiles + tile + 1, :] = near | (far << 16)
        to = place + apart
        to = jnp.where(to >= reps, to - reps, to)
        held = [counted[to * (share // LOW) + k] for k in range(share // LOW)]
        held += [jnp.zeros((tiles, GROUP - share), jnp.float32)] * (share < GROUP)
        held = jnp.concatenate(held, axis=1).astype(jnp.int32)
        ids_ref[3 * tiles // 2 : 2 * tiles, :] = held[: tiles // 2] | (held[tiles // 2 :] << 16)
        ids_ref[2 * tiles : 2 * tiles + 1, :] = jnp.full((1, GROUP), counts_ref[0], jnp.int32)
    for copy in copies[3:]:
        copy.wait()
    values_t = codes_ref[...].T.astype(jnp.float32) * scales_ref[:, pl.ds(first, share)].astype(jnp.float32)
    values_t_ref[...] = values_t
    own_t_ref[...] = values_t.astype(jnp.bfloat16)
    rel_t_ref[...] = relations_ref[...].T


def source_kernel(codes_ref, scales_ref, src_t_ref):
    codes_t = codes_ref[...].T.astype(jnp.float32)
    src_t_ref[...] = (codes_t * scales_ref[...].astype(jnp.float32)).astype(jnp.bfloat16)


def sort_kernel(packing, tiles, share, place_ref, *refs):
    ids_refs, (keys_ref, below_ref, ends_ref, ends_held, sem) = refs[:-5], refs[-5:]
    shards = len(ids_refs)
    first = place_ref[0] * share
    row = lax.broadcasted_iota(jnp.int32, (8, 128), 0)
    lane = lax.broadcasted_iota(jnp.int32, (8, 128), 1)
    keys, ranks, dead = [], [], jnp.zeros((1, 128), jnp.int32)
    for shard, ids_ref in enumerate(ids_refs):
        live = ids_ref[2 * tiles : 2 * tiles + 1, 0:128]
        relations = unpack(ids_ref[tiles : 3 * tiles // 2, :])
        for top in range(0, tiles, 8):
            for left in range(0, GROUP, 128):
                word = ids_ref[top : top + 8, left : left + 128]
                relation = relations[top : top + 8, left : left + 128]
                target = (word >> 16) - first
                target = jnp.where((target >= 0) & (target < share), target, share)
                key = packing.pack(word & 0xFFFF, target, relation, shard * tiles + top + row)
                over = (top + row) * GROUP + left + lane - live
                keys.append(jnp.where(over < 0, key, LAST_KEY))
                ranks.append(jnp.where(over < 0, LAST_KEY, over + dead))
        dead = dead + (tiles * GROUP - live)
    below = [jnp.int32(0)]
    for at in range(1, shards + 1):
        bound = LAST_KEY if at == shards else packing.bound(at * share)
        inside = functools.reduce(jnp.add, [jnp.where(key < bound, 1.0, 0.0) for key in keys])
        below.append(jnp.sum(inside).astype(jnp.int32))
    fill = [(below[at] - below[at + 1]) & (TILE - 1) for at in range(shards)]
    enough = functools.reduce(jnp.add, fill) <= len(keys) * 1024 - below[-1]
    filled = [jnp.int32(0)]
    for at in range(shards):
        filled.append(filled[at] + jnp.where(enough, fill[at], 0))
    for at in range(shards + 1):
        below_ref[at] = below[at] + filled[at]
    parts = []
    for key, rank in zip(keys, ranks):
        for at in range(shards - 2, -1, -1):
            key = jnp.where(rank < filled[at + 1], packing.bound((at + 1) * share) - 1, key)
        parts.append(key)
    parts = sort_columns(parts)
    ends_held[...] = jnp.zeros_like(ends_held)
    ends_held[0:1, :] = parts[0][0:1, :]
    ends_held[1:2, :] = parts[-1][7:8, :]
    copy = pltpu.make_async_copy(ends_held, ends_ref, sem)
    copy.start()
    columns = jnp.concatenate(parts, axis=0).T
    spread = max(1, TILE // columns.shape[1])
    rows = columns.shape[0] // spread
    for k in range(spread):
        keys_ref[:rows, k * columns.shape[1] : (k + 1) * columns.shape[1]] = columns[k * rows : (k + 1) * rows]
    keys_ref[rows:, :] = jnp.full((keys_ref.shape[0] - rows, TILE), LAST_KEY, jnp.int32)
    copy.wait()


def part_kernel(packing, tables, opening, closing, negs, place_ref, below_ref, ends_ref, keys_ref, src_t_ref, rel_t_ref, dst_t_ref, *refs):
    refs = list(refs)
    src_total = refs.pop()
    if closing:
        *refs, coef_ref, query_ref, relation_ref, new_query_ref, new_relation_ref, dst_total = refs
        half_ref, times_ref, before_ref, *given, after_ref, src_grad_ref, dst_grad_ref, coefs_ref = refs
        dst_total[...] = before_ref[...]
        for held, source in zip((coef_ref, query_ref, relation_ref, new_query_ref, new_relation_ref), given):
            held[...] = source[...]
    elif opening:
        *ids_refs, src_grad_ref, dst_total, coef_ref, query_ref, relation_ref, new_query_ref, new_relation_ref, half_ref, times_ref = refs
        half_ref[...] = dst_t_ref[...].T * jnp.bfloat16(0.5)
        tiles = ids_refs[0].shape[0] // 2
        counted = [unpack(ids_ref[3 * tiles // 2 : 2 * tiles, : half_ref.shape[0]]) for ids_ref in ids_refs]
        counted = jnp.concatenate(counted, axis=0).astype(jnp.float32) * (0.5 / negs)
        times_ref[...] = counted.T.astype(times_ref.dtype)
        dst_total[...] = jnp.zeros_like(dst_total)
    else:
        half_ref, times_ref = refs[:2]
        src_grad_ref, dst_total, coef_ref, query_ref, relation_ref, new_query_ref, new_relation_ref = refs[-7:]
    share, width = half_ref.shape

    def span(table):
        at = pick(table, place_ref[0])
        start = pl.multiple_of(at * share, 128)
        begin = below_ref[at] // TILE
        return start, begin, jnp.maximum((below_ref[at + 1] + TILE - 1) // TILE, begin + 1)

    spans = [span(table) for table in tables]
    spans = spans + spans[-1:] * (3 - len(spans))
    start, begin, end = spans[0]
    src_total[...] = jnp.zeros_like(src_total)
    last_row = keys_ref.shape[0] - 9

    def after(at):
        (_, _, end0), (start1, begin1, end1), (start2, begin2, _) = spans
        over, soon, over1 = at + 1 >= end0, at + 2 >= end0, begin1 + 1 >= end1
        one = jnp.where(over, begin1, at + 1)
        two = jnp.where(over, jnp.where(over1, begin2, begin1 + 1), jnp.where(soon, begin1, at + 2))
        two_start = jnp.where(over, jnp.where(over1, start2, start1), jnp.where(soon, start1, start))
        return one, two, pl.multiple_of(two_start, 128)

    def word_of(at):
        return keys_ref[pl.ds(at, 1), :]

    def window(at, start):
        at = jnp.minimum(at, last_row)
        low = packing.source(ends_ref[0, at]) - start
        high = packing.source(ends_ref[1, at + 127 - last_row]) - start
        low = jnp.clip((low >> 7) << 7, 0, share - NARROW)
        return pl.multiple_of(low, 128), jnp.minimum(high, share - 1) - low < NARROW

    def sources(word, start, extent):
        return one_hot(extent, jnp.where(packing.is_empty(word), -1, packing.source(word) - start))

    def query_of(word, start, extent):
        relation = nn_dot(rel_t_ref[...], one_hot(rel_t_ref.shape[1], packing.relation(word)))
        relation = relation.astype(jnp.bfloat16)
        found = nn_dot(src_t_ref[:, pl.ds(start, extent)], sources(word, start, extent))
        return found.astype(jnp.bfloat16) * relation, relation

    def coef_of(word, query):
        times = nn_dot(times_ref[...], one_hot(times_ref.shape[1], packing.block(word)))
        bend = jnp.tanh(nn_dot(half_ref[...], query))
        below = (bend - 1.0).astype(jnp.bfloat16)
        return (times * (bend + 1.0)).astype(jnp.bfloat16) + one_hot(share, packing.target(word), 0.5) * below

    def keep(coef, query, relation, new_query, new_relation):
        coef_ref[...] = coef
        query_ref[...] = query
        relation_ref[...] = relation
        new_query_ref[...] = new_query
        new_relation_ref[...] = new_relation

    if opening:
        query, relation = query_of(word_of(begin), start, share)
        one, _, _ = after(begin)
        one_start = pl.multiple_of(jnp.where(begin + 1 >= end, spans[1][0], start), 128)
        new_query, new_relation = query_of(word_of(one), one_start, share)
        keep(coef_of(word_of(begin), query), query, relation, new_query, new_relation)

    def work(at, one, two, low, two_from, extent):
        coef, query, relation = coef_ref[...], query_ref[...], relation_ref[...]
        new_query, new_relation = new_query_ref[...], new_relation_ref[...]
        back = nn_dot(dst_t_ref[...], coef)
        third_query, third_relation = query_of(word_of(two), two_from, extent)
        new_coef = coef_of(word_of(one), new_query)
        dst_total[...] += nt_dot(coef, query)
        back = back.astype(jnp.bfloat16) * relation
        src_total[pl.ds(low, extent), :] += nt_dot(sources(word_of(at), start + low, extent), back)
        keep(new_coef, new_query, new_relation, third_query, third_relation)

    def light_work(at, one, two, low, two_from, extent):
        coef, query = coef_ref[...], query_ref[...]
        new_query, new_relation = new_query_ref[...], new_relation_ref[...]
        third_query, third_relation = query_of(word_of(two), two_from, extent)
        new_coef = coef_of(word_of(one), new_query)
        dst_total[...] += nt_dot(coef, query)
        coefs_ref[at - begin] = coef
        keep(new_coef, new_query, new_relation, third_query, third_relation)

    def step_with(work):
        def step(at, carry):
            one, two, two_start = after(at)
            if share <= NARROW:
                work(at, one, two, 0, two_start, share)
                return carry
            low, fits = window(at, start)
            two_low, two_fits = window(two, two_start)
            narrow = jnp.logical_and(fits, two_fits)

            @pl.when(narrow)
            def _():
                work(at, one, two, low, pl.multiple_of(two_start + two_low, 128), NARROW)

            @pl.when(jnp.logical_not(narrow))
            def _():
                work(at, one, two, 0, two_start, share)

            return carry

        return step

    light = begin
    if closing:
        light = jnp.minimum(end, begin + HELD)
        lax.fori_loop(begin, light, step_with(light_work), 0)
    lax.fori_loop(light, end, step_with(work), 0)
    src_grad_ref[...] = src_total[...].astype(src_grad_ref.dtype)
    if closing:
        dst_grad_ref[...] = dst_total[...].astype(dst_grad_ref.dtype)


def finish_kernel(packing, owners, place_ref, below_ref, keys_ref, src_grad_ref, rel_t_ref, dst_t_ref, coefs_ref, own_ref, src_total):
    share = own_ref.shape[0]
    at = pick(owners, place_ref[0])
    start = at * share
    begin = below_ref[at] // TILE
    end = jnp.maximum((below_ref[at + 1] + TILE - 1) // TILE, begin + 1)
    src_total[...] = src_grad_ref[...]

    def step(at, carry):
        word = keys_ref[pl.ds(at, 1), :]
        relation = nn_dot(rel_t_ref[...], one_hot(rel_t_ref.shape[1], packing.relation(word)))
        back = (nn_dot(dst_t_ref[...], coefs_ref[at - begin]) * relation).astype(jnp.bfloat16)
        source = one_hot(share, jnp.where(packing.is_empty(word), -1, packing.source(word) - start))
        src_total[...] += nt_dot(source, back)
        return carry

    lax.fori_loop(begin, jnp.minimum(end, begin + HELD), step, 0)
    own_ref[...] = src_total[...].astype(own_ref.dtype)


def update_kernel(place_ref, values_t_ref, scales_ref, accum_ref, arrived_ref, own_ref, returned_ref, piece_ref, low_ref, high_ref, state_ref):
    share = arrived_ref.shape[0]
    first = pl.multiple_of(place_ref[0] * share, 128)
    summed = arrived_ref[...].astype(jnp.float32) + own_ref[...].astype(jnp.float32)
    summed = (summed + returned_ref[...].astype(jnp.float32)).T
    scale = scales_ref[:, pl.ds(first, share)].astype(jnp.float32)
    state = accum_ref[:, pl.ds(first, share)] + jnp.mean(summed * summed, axis=0, keepdims=True)
    updated = values_t_ref[...] - summed * (LEARN_RATE / (jnp.sqrt(state) + ROOT_EPSILON))
    piece = (updated * (1.0 / scale)).T.astype(piece_ref.dtype)
    piece_ref[...] = piece
    low_ref[...] = piece[: share // 2]
    high_ref[...] = piece[share // 2 :]
    state_ref[...] = state


def place_kernel(tables, unit, place_ref, *refs):
    pieces, (out_ref, sems) = refs[: len(tables)], refs[-2:]
    place = place_ref[0]
    for k, (table, chosen) in enumerate(tables):
        row = pl.multiple_of(pick(table, place) * unit, 128)
        copy = pltpu.make_async_copy(pieces[k], out_ref.at[pl.ds(row, pieces[k].shape[0]), :], sems.at[k])
        if chosen is None:
            copy.start()
            continue

        @pl.when(pick(chosen, place) == 1)
        def _(copy=copy):
            copy.start()
            copy.wait()

    for k, (table, chosen) in enumerate(tables):
        if chosen is None:
            row = pl.multiple_of(pick(table, place) * unit, 128)
            pltpu.make_async_copy(pieces[k], out_ref.at[pl.ds(row, pieces[k].shape[0]), :], sems.at[k]).wait()


SMEM = pl.BlockSpec(memory_space=pltpu.SMEM)
VMEM = pl.BlockSpec(memory_space=pltpu.VMEM)


ANY = pl.BlockSpec(memory_space=pl.ANY)
HBM = pl.BlockSpec(memory_space=pltpu.HBM)


def call(kernel, inputs, outs, scratch, name, us, scalars=1, unread=0, aliases={}, scalar_outs=(), in_hbm=0, out=None, grant=VMEM_LIMIT):
    return pl.pallas_call(
        kernel,
        out_shape=outs,
        in_specs=[SMEM] * scalars + [HBM] * in_hbm + [VMEM] * (len(inputs) - scalars - in_hbm - unread) + [ANY] * unread,
        out_specs=out or ([SMEM if at in scalar_outs else VMEM for at in range(len(outs))] if isinstance(outs, tuple) else VMEM),
        scratch_shapes=scratch,
        input_output_aliases=aliases,
        compiler_params=pltpu.CompilerParams(vmem_limit_bytes=grant),
        cost_estimate=pl.CostEstimate(flops=int(us * 1.15e9), bytes_accessed=0, transcendentals=0),
        name=name,
    )(*inputs)


def body(codes, scales, accum, relations, matching, edges, counts, negatives):
    reps = lax.axis_size("rep")
    at_rep = lax.axis_index("rep")
    place = at_rep[None]
    apart_dom = jnp.bitwise_xor(matching[0], lax.axis_index("dom"))
    part_rows, width = codes.shape
    slots = edges.shape[1]
    tiles = slots // GROUP
    negs = negatives.shape[1]
    share = part_rows // reps
    scales_row, accum_row = scales[None], accum[None]

    shape = jax.ShapeDtypeStruct
    ids_shape = shape((2 * tiles + 1, GROUP), jnp.int32)
    *sent, own_t, values_t, rel_t = call(
        functools.partial(open_kernel, tiles, share),
        (place, codes, scales_row, relations, edges, negatives, counts),
        (ids_shape,) * reps
        + (shape((width, share), jnp.bfloat16), shape((width, share), jnp.float32),
           shape(relations.shape[::-1], jnp.bfloat16)),
        [pltpu.VMEM((share, width), codes.dtype), pltpu.VMEM(scales_row.shape, scales.dtype),
         pltpu.VMEM(relations.shape, relations.dtype), pltpu.VMEM(edges.shape, edges.dtype),
         pltpu.VMEM(negatives.shape, negatives.dtype), pltpu.SMEM(counts.shape, counts.dtype),
         pltpu.VMEM((part_rows // LOW, tiles, LOW), jnp.float32), pltpu.SemaphoreType.DMA((6,))],
        "open", 3, in_hbm=6, grant=56 * 1024 * 1024)

    part = shape((share, width), jnp.bfloat16)
    part_sum = shape((share, width), jnp.float32)
    total = pltpu.VMEM((share, width), jnp.float32)
    packing = Packing(part_rows, share, relations.shape[0], reps * tiles)

    @jax.jit
    def sort_edges(place, *ids):
        return call(
            functools.partial(sort_kernel, packing, tiles, share), (place, *ids),
            (shape((reps * slots // TILE + 8, TILE), jnp.int32), shape((reps + 1,), jnp.int32),
             shape((8, 128), jnp.int32)),
            [pltpu.VMEM((8, 128), jnp.int32), pltpu.SemaphoreType.DMA], "sort", 5, scalar_outs=(1, 2),
            grant=40 * 1024 * 1024)

    def gather_edges(place, codes, scales_row, *sent):
        ids = [sent[0]]
        for apart in range(1, reps):
            along = [(at, (at + apart) % reps) for at in range(reps)]
            ids.append(lax.ppermute(sent[apart], "rep", along))
        src_t = call(source_kernel, (codes, scales_row), shape((width, part_rows), jnp.bfloat16), [], "source", 2, scalars=0)
        return (src_t, *ids) + tuple(sort_edges(place, *ids))

    dst_t, src_t, *ids, keys, below, ends = swap_beside(
        apart_dom, own_t, gather_edges, place, codes, scales_row, *sent)

    order = ring_order(reps)
    forward = [(order[i], order[(i + 1) % reps]) for i in range(reps)]

    def owners(behind):
        return [order[(order.index(z) - behind) % reps] for z in range(reps)]

    wide = shape((share, TILE), jnp.bfloat16)
    tall = shape((width, TILE), jnp.bfloat16)
    state = [wide, tall, tall, tall, tall]
    moving = arrived = None
    for behind in range(1, reps + 1):
        opening, closing = behind == 1, behind == reps
        table = owners(behind)
        chain = [owners(later) for later in range(behind, min(behind + 2, reps) + 1)]
        kept = shape((HELD, share, TILE), jnp.bfloat16)
        outs = (part_sum, part, kept) if closing else (part, part_sum, *state)
        scratch = ([pltpu.VMEM(kept.shape, kept.dtype) for kept in state] + [total] if closing else []) + [total]
        if opening:
            given = tuple(ids)
            outs += (part, shape((share, reps * tiles), jnp.bfloat16))
        else:
            given = (half, times, dst_grad) + held + (arrived if arrived is not None else below,)
        done = call(
            functools.partial(part_kernel, packing, chain, opening, closing, negs),
            (place, below, ends, keys, src_t, rel_t, dst_t) + given, outs, scratch, "part", 9,
            scalars=3, unread=0 if opening else 1,
            aliases={} if opening or closing else {9 + k: 1 + k for k in range(6)})
        src_grad, dst_grad = done[:2]
        held = tuple(done[2:7])
        if opening:
            half, times = done[7:]
            moving = src_grad
        elif not closing:
            arrived = lax.ppermute(moving, "rep", forward)
            moving = (arrived.astype(jnp.float32) + src_grad.astype(jnp.float32)).astype(jnp.bfloat16)
    arrived = lax.ppermute(moving, "rep", forward)
    @jax.jit
    def finish(*given):
        return call(functools.partial(finish_kernel, packing, table), given, part, [total], "finish", 3, scalars=2)

    returned, own = swap_beside(
        apart_dom, dst_grad, lambda *given: (finish(*given),), place, below, keys, src_grad, rel_t, dst_t, done[2])

    half_part = shape((share // 2, width), jnp.bfloat16)
    piece, low, high, state = call(
        update_kernel, (place, values_t, scales_row, accum_row, arrived, own, returned),
        (part, half_part, half_part, shape((1, share), jnp.float32)), [], "update", 2)

    def put(tables, pieces, given, us):
        return call(
            functools.partial(place_kernel, tables, share // 2), (place, *pieces) + given, shape(codes.shape, jnp.bfloat16),
            [pltpu.SemaphoreType.DMA((len(pieces),))], "place", us, unread=len(given),
            aliases={1 + len(pieces): 0} if given else {}, out=HBM)

    if reps == 4:
        across = [(0, 2), (2, 0), (1, 3), (3, 1)]
        far = [lax.ppermute(held, "rep", across) for held in (low, high)]
        near = lax.ppermute(piece, "rep", [(0, 1), (1, 0), (2, 3), (3, 2)])
        middle = lax.ppermute(piece, "rep", [(1, 2), (2, 1)])
        ends = [lax.ppermute(held, "rep", [(2, 3), (1, 0)]) for held in far]
        early = [(piece, ([0, 2, 4, 6], None)), (near, ([2, 0, 6, 4], None))]
        early += [(held, ([4 + k, 6 + k, k, 2 + k], None)) for k, held in enumerate(far)]
        late = [(middle, ([6, 4, 2, 0], [0, 1, 1, 0]))]
        late += [(held, ([6 + k, 4 + k, 2 + k, k], [1, 0, 0, 1])) for k, held in enumerate(ends)]
    else:
        pieces = [piece]
        for behind in range(1, reps):
            pieces.append(lax.ppermute(pieces[-1], "rep", forward))
        early = [(held, ([2 * at for at in owners(behind)], None)) for behind, held in enumerate(pieces)]
        early, late = early[:-1], early[-1:]
    new_codes = put([table for _, table in early], [held for held, _ in early], (), 1)
    new_codes = put([table for _, table in late], [held for held, _ in late], (new_codes,), 1)
    return (new_codes, state[0])


def solution(mesh):
    placed = (
        P("dom", None),
        P("dom"),
        P("dom"),
        P(),
        P("dom"),
        P(None, ("dom", "rep")),
        P(("dom", "rep")),
        P(("dom", "rep"), None),
    )
    return jax.shard_map(
        body,
        mesh=mesh,
        in_specs=placed,
        out_specs=(P("dom", None), P(("dom", "rep"))),
        check_vma=False,
    )
```

time: 599 us -> 84.5 us (0.14)
  starting transfers between devices: 188 us -> 17.8 us
  waiting for transfers between devices: 186 us -> 20.3 us
  other arithmetic: 96 us -> 0.13 us
  local copies, waits for them, and re-layouts: 68.9 us -> 0.71 us
  Pallas kernels: 0 us -> 44.4 us
  matrix products: 34.3 us -> 0 us
  between operations: 15.5 us -> 2.26 us
  loops' own time: 6.4 us -> 0.12 us
    ppermute x6 -> x14, starting transfers between devices: 188 us -> 17.8 us  [the longest x3 7.01 us: gather_edges(): ids.append(lax.ppermute(sent[apart], 'rep', along))]
    psum x1 -> x0, waiting for transfers between devices: 88.1 us -> none  [body(): summed = lax.psum(src_grad + returned, 'rep')]
    ppermute x6 -> x14, waiting for transfers between devices: 98.1 us -> 20.3 us  [the longest x2 10.2 us: body(): far = [lax.ppermute(held, 'rep', across) for held in (low, high)]]
    scatter-add x12 -> x0, other arithmetic: 73.1 us -> none  [the longest x8 47.5 us: score_group(): grads_in[1].at[block_ids[2]].add(target_grad).at[block_negs]]
    gather x20 -> x0, local copies, waits for them, and re-layouts: 46.2 us -> none  [the longest x4 19.9 us: group_terms(): negative_rows = jnp.take(dst_block, negative_ids, axis=0)]
    pallas_call x0 -> x11, Pallas kernels: none -> 44.4 us  [call(): pl.pallas_call(kernel, out_shape=outs, in_specs=[SMEM] * scalars + [HBM]...]
    dot_general x16 -> x0, matrix products: 34.3 us -> none  [the longest x4 10.8 us: group_terms(): lax.dot_general(neg_coef, query, (((0,), (0,)), ((), ())), preferred_elem...]
    mul x8 -> x0, local copies, waits for them, and re-layouts: 16.3 us -> none  [the longest x4 8.2 us: group_terms(): source_grad = query_grad * relation_rows]
  transfers between devices with their start and end apart: 7 -> 14, of which waited for: 7 -> 9; matrix products, arithmetic and copies ran while one was open for 0% -> 0% of each run, Pallas kernels for 0% -> 36%
where the time goes in v1:
time: 84.5 us; the launch traced here: 85.7 us
  Pallas kernels  44.4 us (53%)
  waiting for transfers between devices  20.3 us (24%)
  starting transfers between devices  17.8 us (21%)
  between operations  2.26 us (3%)
    pallas_call x11, Pallas kernels, call(): pl.pallas_call(kernel, out_shape=outs, in_specs=[SMEM] * scalars + [HBM]...  44.4 us
    ppermute x2, waiting for transfers between devices, body(): far = [lax.ppermute(held, 'rep', across) for held in (low, high)]  10.2 us
    ppermute x3, starting transfers between devices, gather_edges(): ids.append(lax.ppermute(sent[apart], 'rep', along))  7.01 us
    ppermute x2, waiting for transfers between devices, body(): ends = [lax.ppermute(held, 'rep', [(2, 3), (1, 0)]) for held in far]  4.63 us
    ppermute x3, starting transfers between devices, body(): arrived = lax.ppermute(moving, 'rep', forward)  3.09 us
    ppermute x2, starting transfers between devices, body(): far = [lax.ppermute(held, 'rep', across) for held in (low, high)]  2.92 us
    ppermute x2, starting transfers between devices, body(): ends = [lax.ppermute(held, 'rep', [(2, 3), (1, 0)]) for held in far]  2.56 us
    ppermute x3, waiting for transfers between devices, gather_edges(): ids.append(lax.ppermute(sent[apart], 'rep', along))  2.42 us
  transfers between devices with their start and end apart: 14, of which 9 were waited for; matrix products, arithmetic and copies ran while one was open for 0% of the time, Pallas kernels for 36%

profile of v1, /device:TPU:0, one launch (start us, length us, event | category | flops | bytes accessed | tf_op | source)
XLA Modules:
  0.0 85.7 jit_solution(11873108562694739034)
XLA Ops:
  1.9 0.7 broadcast_in_dim.10.scales_hbm.scales_ref
  2.6 2.6 %open.1 = (s32[17,512]{1,0:T(8,128)S(1)}, s32[17,512]{1,0:T(8,128)S(1)}, s32[17,512]{1,0:T(8,128)S(1)}, s32[17,512]{1,0:T(8,128)S(1)}, bf16[256,512]{1,0:T(8,128...) custom-call(s32[1]{0:T(128)} %bitcast.place_ref, bf16[2048,256]{1,0:T(8,128)(2,1)} %codes_hbm.1, ...), custom_call_target="tpu_custom_call" | custom-call | flops 3449999872 | tf_op jit(solution)/shard_map/open/pallas_call | solution.py:483
  5.2 15.7 %conditional.2 = (bf16[256,512]{1,0:T(8,128)(2,1)}, bf16[256,2048]{1,0:T(8,128)(2,1)S(1)}, s32[17,512]{1,0:T(8,128)}, s32[17,512]{1,0:T(8,128)}, s32[17,512]{1,0...) conditional(s32[]{:T(128)} %clamp.4, ...), branch_computations={%region_0.1_spmd, %region_1.2_spmd, %region_2.3_spmd, %region_3.4_... | conditional | flops 8049999872 | bytes 1466592 | solution.py:32
  5.3 3.1 %collective-permute-start.9 = (s32[17,512]{1,0:T(8,128)S(1)}, s32[17,512]{1,0:T(8,128)}, u32[]{:S(2)}, u32[]{:S(2)}) collective-permute-start(s32[17,512]{1,0:T(8,128)S(1)} %get-tuple-element.249), channel_id=1, source_target_pairs={{0,1},{1,2},{2,3},{3,0},{4,5},{5,6},{6,7},{7,4},{8,9},{9,10},{10,1... | collective-permute-start | bytes 104456 | tf_op jit(solution)/shard_map/cond/branch_2_fun/ppermute | solution.py:540
  8.3 2.6 %collective-permute-start.10 = (s32[17,512]{1,0:T(8,128)S(1)}, s32[17,512]{1,0:T(8,128)}, u32[]{:S(2)}, u32[]{:S(2)}) collective-permute-start(s32[17,512]{1,0:T(8,128)S(1)} %get-tuple-element.250), channel_id=1, source_target_pairs={{0,2},{1,3},{2,0},{3,1},{4,6},{5,7},{6,4},{7,5},{8,10},{9,11},{10,... | collective-permute-start | bytes 104456 | tf_op jit(solution)/shard_map/cond/branch_2_fun/ppermute | solution.py:540
  10.9 1.3 %collective-permute-start.11 = (s32[17,512]{1,0:T(8,128)S(1)}, s32[17,512]{1,0:T(8,128)}, u32[]{:S(2)}, u32[]{:S(2)}) collective-permute-start(s32[17,512]{1,0:T(8,128)S(1)} %get-tuple-element.251), channel_id=1, source_target_pairs={{0,3},{1,0},{2,1},{3,2},{4,7},{5,4},{6,5},{7,6},{8,11},{9,8},{10,9... | collective-permute-start | bytes 104456 | tf_op jit(solution)/shard_map/cond/branch_2_fun/ppermute | solution.py:540
  12.7 1.9 %collective-permute-done.10.refs_2_ = s32[17,512]{1,0:T(8,128)} collective-permute-done((s32[17,512]{1,0:T(8,128)S(1)}, s32[17,512]{1,0:T(8,128)}, u32[]{:S(2)}, u32[]{:S(2)}) %collective-permute-start.10) | collective-permute-done | bytes 34848 | tf_op jit(solution)/shard_map/cond/branch_2_fun/ppermute | solution.py:540
  15.1 5.0 %sort.9 = (s32[40,512]{1,0:T(8,128)S(1)}, s32[5]{0:T(128)S(1)}, s32[8,128]{1,0:T(8,128)S(1)}) custom-call(s32[1]{0:T(128)} %get-tuple-element.252.place_ref, s32[17,512]{1,0:T(8,128)S(1)} %get-tuple-element.253.refs_0_, s32[17,512]{1,0:T(8,128)} %collective-permute-done.9.refs_1_, s32[17,512]{1,0:T(8,128)} %collective-permute-done.10.refs_2_, ...), custom_call_target="tpu_custom_call" | custom-call | flops 5750000128 | tf_op jit(solution)/shard_map/cond/branch_2_fun/jit(sort_edges)/sort/pallas_call | solution.py:483
  20.1 0.8 collective-permute-done.8
  20.9 7.9 %part.4 = (bf16[512,256]{1,0:T(8,128)(2,1)S(1)}, f32[512,256]{1,0:T(8,128)S(1)}, bf16[512,512]{1,0:T(8,128)(2,1)S(1)}, bf16[256,512]{1,0:T(8,128)(2,1)S(1)}, bf1...) custom-call(s32[1]{0:T(128)} %bitcast.place_ref, ...), custom_call_target="tpu_custom_call" | custom-call | flops 10350000128 | tf_op jit(solution)/shard_map/part/pallas_call | solution.py:483
  29.4 6.9 %part.5 = (bf16[512,256]{1,0:T(8,128)(2,1)S(1)}, f32[512,256]{1,0:T(8,128)S(1)}, bf16[512,512]{1,0:T(8,128)(2,1)S(1)}, bf16[256,512]{1,0:T(8,128)(2,1)S(1)}, bf1...) custom-call(s32[1]{0:T(128)} %bitcast.place_ref, ...), custom_call_target="tpu_custom_call", output_to_operand_aliasing={{1}: (9, {}), {2}: (10, {}), {3}: (11, {}), {4}: (12, {}), ... | custom-call | flops 10350000128 | tf_op jit(solution)/shard_map/part/pallas_call | solution.py:483
  36.3 0.9 %collective-permute-done.35.refs_8_ = bf16[512,256]{1,0:T(8,128)(2,1)S(1)} collective-permute-done((bf16[512,256]{1,0:T(8,128)(2,1)S(1)}, bf16[512,256]{1,0:T(8,128)(2,1)S(1)}, u32[]{:S(2)}, u32[]{:S(2)}) %collective-permute-start.35) | collective-permute-done | bytes 262176 | tf_op jit(solution)/shard_map/ppermute | solution.py:580
  37.3 1.8 %collective-permute-start.36 = (bf16[512,256]{1,0:T(8,128)(2,1)S(1)}, bf16[512,256]{1,0:T(8,128)(2,1)S(1)}, u32[]{:S(2)}, u32[]{:S(2)}) collective-permute-start(bf16[512,256]{1,0:T(8,128)(2,1)S(1)} %add_convert_fusion.1), channel_id=1, source_target_pairs={{0,2},{2,3},{3,1},{1,0},{4,6},{6,7},{7,5},{5,4},{8,10},{10,11},{11... | collective-permute-start | bytes 786440 | tf_op jit(solution)/shard_map/ppermute | solution.py:580
  39.1 6.9 %part.6 = (bf16[512,256]{1,0:T(8,128)(2,1)S(1)}, f32[512,256]{1,0:T(8,128)S(1)}, bf16[512,512]{1,0:T(8,128)(2,1)S(1)}, bf16[256,512]{1,0:T(8,128)(2,1)S(1)}, bf1...) custom-call(s32[1]{0:T(128)} %bitcast.place_ref, ...), custom_call_target="tpu_custom_call", output_to_operand_aliasing={{1}: (9, {}), {2}: (10, {}), {3}: (11, {}), {4}: (12, {}), ... | custom-call | flops 10350000128 | tf_op jit(solution)/shard_map/part/pallas_call | solution.py:483
  46.1 0.8 collective-permute-start.37
  46.8 5.7 %part.7 = (f32[512,256]{1,0:T(8,128)S(1)}, bf16[512,256]{1,0:T(8,128)(2,1)S(1)}, bf16[10,512,512]{2,1,0:T(8,128)(2,1)S(1)}) custom-call(s32[1]{0:T(128)} %bitcast.place_ref, s32[5]{0:T(128)S(1)} %get-tuple-element.412.below_ref.refs_8_, s32[8,128]{1,0:T(8,128)S(1)} %get-tuple-element.413.ends_ref, s32[40,512]{1,0:T(8,128)S(1)} %get-tuple-element.414.keys_ref, ...), custom_call_target="tpu_custom_call" | custom-call | flops 10350000128 | tf_op jit(solution)/shard_map/part/pallas_call | solution.py:483
  52.6 6.3 %conditional.3 = (bf16[512,256]{1,0:T(8,128)(2,1)}, bf16[512,256]{1,0:T(8,128)(2,1)S(1)}) conditional(s32[]{:T(128)} %clamp.4, (bf16[512,256]{1,0:T(8,128)(2,1)S(1)}, s32[1]{0:T(128)}, s32[5]{0:T(128)S(1)}, s32[40,512]{1,0:T(8,128)S(1)}, f32[512,256]{1,0:T(8,128)S(1)}, /*index=5*/bf16[256,64]{1,0:T(8,128)(2,1)S(1)}, ...), branch_computations={%region_7.8_spmd, %region_8.9_spmd, %region_9.10_spmd, %region_10.... | conditional | flops 3449999872 | bytes 1048632 | solution.py:32
  52.7 4.8 %finish.9 = bf16[512,256]{1,0:T(8,128)(2,1)S(1)} custom-call(s32[1]{0:T(128)} %get-tuple-element.318.place_ref, s32[5]{0:T(128)S(1)} %get-tuple-element.319.below_ref, s32[40,512]{1,0:T(8,128)S(1)} %get-tuple-element.320.keys_ref, f32[512,256]{1,0:T(8,128)S(1)} %get-tuple-element.321.src_grad_ref, bf16[256,64]{1,0:T(8,128)(2,1)S(1)} %get-tuple-element.322.rel_t_ref, ...), custom_call_target="tpu_custom_call" | custom-call | flops 3449999872 | tf_op jit(solution)/shard_map/cond/branch_2_fun/jit(finish)/finish/pallas_call | solution.py:483
  57.6 1.3 %collective-permute-done.30 = bf16[512,256]{1,0:T(8,128)(2,1)} collective-permute-done((bf16[512,256]{1,0:T(8,128)(2,1)S(1)}, bf16[512,256]{1,0:T(8,128)(2,1)}, u32[]{:S(2)}, u32[]{:S(2)}) %collective-permute-start.30) | collective-permute-done | bytes 262176 | tf_op jit(solution)/shard_map/cond/branch_2_fun/ppermute | solution.py:30
  58.9 1.9 %update.1 = (bf16[512,256]{1,0:T(8,128)(2,1)S(1)}, bf16[256,256]{1,0:T(8,128)(2,1)S(1)}, bf16[256,256]{1,0:T(8,128)(2,1)S(1)}, f32[1,512]{1,0:T(1,128)}) custom-call(s32[1]{0:T(128)} %bitcast.place_ref, f32[256,512]{1,0:T(8,128)S(1)} %copy-done.1, bf16[1,2048]{1,0:T(2,128)(2,1)S(1)} %broadcast_in_dim.10.scales_hbm.scales_ref, f32[1,2048]{1,0:T(1,128)S(1)} %bitcast.5, ...), custom_call_target="tpu_custom_call" | custom-call | flops 2300000000 | tf_op jit(solution)/shard_map/update/pallas_call | solution.py:483
  60.8 1.4 %collective-permute-start.43 = (bf16[512,256]{1,0:T(8,128)(2,1)S(1)}, bf16[512,256]{1,0:T(8,128)(2,1)S(1)}, u32[]{:S(2)}, u32[]{:S(2)}) collective-permute-start(bf16[512,256]{1,0:T(8,128)(2,1)S(1)} %get-tuple-element.449.refs_0_), channel_id=1, source_target_pairs={{0,1},{1,0},{2,3},{3,2},{4,5},{5,4},{6,7},{7,6},{8,9},{9,8},{10,11... | collective-permute-start | bytes 786440 | tf_op jit(solution)/shard_map/ppermute | solution.py:604
  62.2 1.9 %collective-permute-start.39 = (bf16[256,256]{1,0:T(8,128)(2,1)S(1)}, bf16[256,256]{1,0:T(8,128)(2,1)S(1)}, u32[]{:S(2)}, u32[]{:S(2)}) collective-permute-start(bf16[256,256]{1,0:T(8,128)(2,1)S(1)} %get-tuple-element.450), channel_id=1, source_target_pairs={{0,2},{2,0},{1,3},{3,1},{4,6},{6,4},{5,7},{7,5},{8,10},{10,8},{9,1... | collective-permute-start | bytes 393224 | tf_op jit(solution)/shard_map/ppermute | solution.py:603
  64.0 1.1 %collective-permute-start.41 = (bf16[256,256]{1,0:T(8,128)(2,1)S(1)}, bf16[256,256]{1,0:T(8,128)(2,1)S(1)}, u32[]{:S(2)}, u32[]{:S(2)}) collective-permute-start(bf16[256,256]{1,0:T(8,128)(2,1)S(1)} %get-tuple-element.451), channel_id=1, source_target_pairs={{0,2},{2,0},{1,3},{3,1},{4,6},{6,4},{5,7},{7,5},{8,10},{10,8},{9,1... | collective-permute-start | bytes 393224 | tf_op jit(solution)/shard_map/ppermute | solution.py:603
  65.1 0.7 collective-permute-start.38
  65.8 8.7 %collective-permute-done.39.refs_2_ = bf16[256,256]{1,0:T(8,128)(2,1)S(1)} collective-permute-done((bf16[256,256]{1,0:T(8,128)(2,1)S(1)}, bf16[256,256]{1,0:T(8,128)(2,1)S(1)}, u32[]{:S(2)}, u32[]{:S(2)}) %collective-permute-start.39) | collective-permute-done | bytes 131104 | tf_op jit(solution)/shard_map/ppermute | solution.py:603
  74.5 1.3 %collective-permute-start.40 = (bf16[256,256]{1,0:T(8,128)(2,1)S(1)}, bf16[256,256]{1,0:T(8,128)(2,1)S(1)}, u32[]{:S(2)}, u32[]{:S(2)}) collective-permute-start(bf16[256,256]{1,0:T(8,128)(2,1)S(1)} %collective-permute-done.39.refs_2_), channel_id=1, source_target_pairs={{2,3},{1,0},{6,7},{5,4},{10,11},{9,8},{14,15},{13,12},{18,19},{17,... | collective-permute-start | bytes 393224 | tf_op jit(solution)/shard_map/ppermute | solution.py:606
  75.8 1.5 %collective-permute-done.41.refs_3_ = bf16[256,256]{1,0:T(8,128)(2,1)S(1)} collective-permute-done((bf16[256,256]{1,0:T(8,128)(2,1)S(1)}, bf16[256,256]{1,0:T(8,128)(2,1)S(1)}, u32[]{:S(2)}, u32[]{:S(2)}) %collective-permute-start.41) | collective-permute-done | bytes 131104 | tf_op jit(solution)/shard_map/ppermute | solution.py:603
  77.3 1.3 %collective-permute-start.42 = (bf16[256,256]{1,0:T(8,128)(2,1)S(1)}, bf16[256,256]{1,0:T(8,128)(2,1)S(1)}, u32[]{:S(2)}, u32[]{:S(2)}) collective-permute-start(bf16[256,256]{1,0:T(8,128)(2,1)S(1)} %collective-permute-done.41.refs_3_), channel_id=1, source_target_pairs={{2,3},{1,0},{6,7},{5,4},{10,11},{9,8},{14,15},{13,12},{18,19},{17,... | collective-permute-start | bytes 393224 | tf_op jit(solution)/shard_map/ppermute | solution.py:606
  78.6 0.9 %place.2.refs_3_ = bf16[2048,256]{1,0:T(8,128)(2,1)} custom-call(s32[1]{0:T(128)} %bitcast.place_ref, bf16[512,256]{1,0:T(8,128)(2,1)S(1)} %get-tuple-element.449.refs_0_, bf16[512,256]{1,0:T(8,128)(2,1)S(1)} %collective-permute-done.43.refs_1_, bf16[256,256]{1,0:T(8,128)(2,1)S(1)} %collective-permute-done.39.refs_2_, ...), custom_call_target="tpu_custom_call" | custom-call | flops 1150000000 | tf_op jit(solution)/shard_map/place/pallas_call | solution.py:483
  79.5 1.8 %collective-permute-done.40.refs_1_ = bf16[256,256]{1,0:T(8,128)(2,1)S(1)} collective-permute-done((bf16[256,256]{1,0:T(8,128)(2,1)S(1)}, bf16[256,256]{1,0:T(8,128)(2,1)S(1)}, u32[]{:S(2)}, u32[]{:S(2)}) %collective-permute-start.40) | collective-permute-done | bytes 131104 | tf_op jit(solution)/shard_map/ppermute | solution.py:606
  81.3 2.8 %collective-permute-done.42.refs_2_ = bf16[256,256]{1,0:T(8,128)(2,1)S(1)} collective-permute-done((bf16[256,256]{1,0:T(8,128)(2,1)S(1)}, bf16[256,256]{1,0:T(8,128)(2,1)S(1)}, u32[]{:S(2)}, u32[]{:S(2)}) %collective-permute-start.42) | collective-permute-done | bytes 131104 | tf_op jit(solution)/shard_map/ppermute | solution.py:606
  84.1 1.3 %place.3 = bf16[2048,256]{1,0:T(8,128)(2,1)} custom-call(s32[1]{0:T(128)} %bitcast.place_ref, bf16[512,256]{1,0:T(8,128)(2,1)S(1)} %collective-permute-done.38.refs_0_, bf16[256,256]{1,0:T(8,128)(2,1)S(1)} %collective-permute-done.40.refs_1_, bf16[256,256]{1,0:T(8,128)(2,1)S(1)} %collective-permute-done.42.refs_2_, ...), custom_call_target="tpu_custom_call", output_to_operand_aliasing={{}: (4, {})} | custom-call | flops 1150000000 | tf_op jit(solution)/shard_map/place/pallas_call | solution.py:483
  (18 shorter events, 1.7 us)
Async XLA Ops:
  2.6 2.6 %copy-start.2 = (bf16[2048,256]{1,0:T(8,128)(2,1)S(1)}, bf16[2048,256]{1,0:T(8,128)(2,1)}, u32[]{:S(2)}) copy-start(bf16[2048,256]{1,0:T(8,128)(2,1)} %codes_hbm.1) | copy-start | bytes 3145732
  5.3 7.5 %collective-permute-start.9 = (s32[17,512]{1,0:T(8,128)S(1)}, s32[17,512]{1,0:T(8,128)}, u32[]{:S(2)}, u32[]{:S(2)}) collective-permute-start(s32[17,512]{1,0:T(8,128)S(1)} %get-tuple-element.249), channel_id=1, source_target_pairs={{0,1},{1,2},{2,3},{3,0},{4,5},{5,6},{6,7},{7,4},{8,9},{9,10},{10,1... | collective-permute-start | bytes 104456 | tf_op jit(solution)/shard_map/cond/branch_2_fun/ppermute | solution.py:540
  8.3 6.3 %collective-permute-start.10 = (s32[17,512]{1,0:T(8,128)S(1)}, s32[17,512]{1,0:T(8,128)}, u32[]{:S(2)}, u32[]{:S(2)}) collective-permute-start(s32[17,512]{1,0:T(8,128)S(1)} %get-tuple-element.250), channel_id=1, source_target_pairs={{0,2},{1,3},{2,0},{3,1},{4,6},{5,7},{6,4},{7,5},{8,10},{9,11},{10,... | collective-permute-start | bytes 104456 | tf_op jit(solution)/shard_map/cond/branch_2_fun/ppermute | solution.py:540
  10.9 4.2 %collective-permute-start.11 = (s32[17,512]{1,0:T(8,128)S(1)}, s32[17,512]{1,0:T(8,128)}, u32[]{:S(2)}, u32[]{:S(2)}) collective-permute-start(s32[17,512]{1,0:T(8,128)S(1)} %get-tuple-element.251), channel_id=1, source_target_pairs={{0,3},{1,0},{2,1},{3,2},{4,7},{5,4},{6,5},{7,6},{8,11},{9,8},{10,9... | collective-permute-start | bytes 104456 | tf_op jit(solution)/shard_map/cond/branch_2_fun/ppermute | solution.py:540
  12.3 8.7 %collective-permute-start.8 = (bf16[256,512]{1,0:T(8,128)(2,1)S(1)}, bf16[256,512]{1,0:T(8,128)(2,1)}, u32[]{:S(2)}, u32[]{:S(2)}) collective-permute-start(bf16[256,512]{1,0:T(8,128)(2,1)S(1)} %get-tuple-element.246), channel_id=1, source_target_pairs={{0,12},{4,8},{8,4},{12,0},{16,28},{20,24},{24,20},{28,16},{1,13},{... | collective-permute-start | bytes 786440 | tf_op jit(solution)/shard_map/cond/branch_2_fun/ppermute | solution.py:30
  28.9 8.4 %collective-permute-start.35 = (bf16[512,256]{1,0:T(8,128)(2,1)S(1)}, bf16[512,256]{1,0:T(8,128)(2,1)S(1)}, u32[]{:S(2)}, u32[]{:S(2)}) collective-permute-start(bf16[512,256]{1,0:T(8,128)(2,1)S(1)} %get-tuple-element.421), channel_id=1, source_target_pairs={{0,2},{2,3},{3,1},{1,0},{4,6},{6,7},{7,5},{5,4},{8,10},{10,11},{11... | collective-permute-start | bytes 786440 | tf_op jit(solution)/shard_map/ppermute | solution.py:580
  37.3 8.7 %collective-permute-start.36 = (bf16[512,256]{1,0:T(8,128)(2,1)S(1)}, bf16[512,256]{1,0:T(8,128)(2,1)S(1)}, u32[]{:S(2)}, u32[]{:S(2)}) collective-permute-start(bf16[512,256]{1,0:T(8,128)(2,1)S(1)} %add_convert_fusion.1), channel_id=1, source_target_pairs={{0,2},{2,3},{3,1},{1,0},{4,6},{6,7},{7,5},{5,4},{8,10},{10,11},{11... | collective-permute-start | bytes 786440 | tf_op jit(solution)/shard_map/ppermute | solution.py:580
  46.1 12.8 %collective-permute-start.37 = (bf16[512,256]{1,0:T(8,128)(2,1)S(1)}, bf16[512,256]{1,0:T(8,128)(2,1)S(1)}, u32[]{:S(2)}, u32[]{:S(2)}) collective-permute-start(bf16[512,256]{1,0:T(8,128)(2,1)S(1)} %add_convert_fusion), channel_id=1, source_target_pairs={{0,2},{2,3},{3,1},{1,0},{4,6},{6,7},{7,5},{5,4},{8,10},{10,11},{11... | collective-permute-start | bytes 786440 | tf_op jit(solution)/shard_map/ppermute | solution.py:582
  52.6 6.3 %copy-start = (f32[2048]{0:T(1024)S(1)}, f32[2048]{0:T(1024)}, u32[]{:S(2)}) copy-start(f32[2048]{0:T(1024)} %param.24) | copy-start | bytes 24580
  52.6 6.3 %copy-start.1 = (f32[256,512]{1,0:T(8,128)S(1)}, f32[256,512]{1,0:T(8,128)}, u32[]{:S(2)}) copy-start(f32[256,512]{1,0:T(8,128)} %get-tuple-element.406.values_t_ref) | copy-start | bytes 1572868
  52.6 6.2 %collective-permute-start.30 = (bf16[512,256]{1,0:T(8,128)(2,1)S(1)}, bf16[512,256]{1,0:T(8,128)(2,1)}, u32[]{:S(2)}, u32[]{:S(2)}) collective-permute-start(bf16[512,256]{1,0:T(8,128)(2,1)S(1)} %get-tuple-element.317), channel_id=1, source_target_pairs={{0,12},{4,8},{8,4},{12,0},{16,28},{20,24},{24,20},{28,16},{1,13},{... | collective-permute-start | bytes 786440 | tf_op jit(solution)/shard_map/cond/branch_2_fun/ppermute | solution.py:30
  60.8 17.7 %collective-permute-start.43 = (bf16[512,256]{1,0:T(8,128)(2,1)S(1)}, bf16[512,256]{1,0:T(8,128)(2,1)S(1)}, u32[]{:S(2)}, u32[]{:S(2)}) collective-permute-start(bf16[512,256]{1,0:T(8,128)(2,1)S(1)} %get-tuple-element.449.refs_0_), channel_id=1, source_target_pairs={{0,1},{1,0},{2,3},{3,2},{4,5},{5,4},{6,7},{7,6},{8,9},{9,8},{10,11... | collective-permute-start | bytes 786440 | tf_op jit(solution)/shard_map/ppermute | solution.py:604
  62.2 12.3 %collective-permute-start.39 = (bf16[256,256]{1,0:T(8,128)(2,1)S(1)}, bf16[256,256]{1,0:T(8,128)(2,1)S(1)}, u32[]{:S(2)}, u32[]{:S(2)}) collective-permute-start(bf16[256,256]{1,0:T(8,128)(2,1)S(1)} %get-tuple-element.450), channel_id=1, source_target_pairs={{0,2},{2,0},{1,3},{3,1},{4,6},{6,4},{5,7},{7,5},{8,10},{10,8},{9,1... | collective-permute-start | bytes 393224 | tf_op jit(solution)/shard_map/ppermute | solution.py:603
  64.0 13.2 %collective-permute-start.41 = (bf16[256,256]{1,0:T(8,128)(2,1)S(1)}, bf16[256,256]{1,0:T(8,128)(2,1)S(1)}, u32[]{:S(2)}, u32[]{:S(2)}) collective-permute-start(bf16[256,256]{1,0:T(8,128)(2,1)S(1)} %get-tuple-element.451), channel_id=1, source_target_pairs={{0,2},{2,0},{1,3},{3,1},{4,6},{6,4},{5,7},{7,5},{8,10},{10,8},{9,1... | collective-permute-start | bytes 393224 | tf_op jit(solution)/shard_map/ppermute | solution.py:603
  65.1 19.0 %collective-permute-start.38 = (bf16[512,256]{1,0:T(8,128)(2,1)S(1)}, bf16[512,256]{1,0:T(8,128)(2,1)S(1)}, u32[]{:S(2)}, u32[]{:S(2)}) collective-permute-start(bf16[512,256]{1,0:T(8,128)(2,1)S(1)} %get-tuple-element.449.refs_0_), channel_id=1, source_target_pairs={{1,2},{2,1},{5,6},{6,5},{9,10},{10,9},{13,14},{14,13},{17,18},{18,... | collective-permute-start | bytes 786440 | tf_op jit(solution)/shard_map/ppermute | solution.py:605
  74.5 6.8 %collective-permute-start.40 = (bf16[256,256]{1,0:T(8,128)(2,1)S(1)}, bf16[256,256]{1,0:T(8,128)(2,1)S(1)}, u32[]{:S(2)}, u32[]{:S(2)}) collective-permute-start(bf16[256,256]{1,0:T(8,128)(2,1)S(1)} %collective-permute-done.39.refs_2_), channel_id=1, source_target_pairs={{2,3},{1,0},{6,7},{5,4},{10,11},{9,8},{14,15},{13,12},{18,19},{17,... | collective-permute-start | bytes 393224 | tf_op jit(solution)/shard_map/ppermute | solution.py:606
  77.3 6.8 %collective-permute-start.42 = (bf16[256,256]{1,0:T(8,128)(2,1)S(1)}, bf16[256,256]{1,0:T(8,128)(2,1)S(1)}, u32[]{:S(2)}, u32[]{:S(2)}) collective-permute-start(bf16[256,256]{1,0:T(8,128)(2,1)S(1)} %collective-permute-done.41.refs_3_), channel_id=1, source_target_pairs={{2,3},{1,0},{6,7},{5,4},{10,11},{9,8},{14,15},{13,12},{18,19},{17,... | collective-permute-start | bytes 393224 | tf_op jit(solution)/shard_map/ppermute | solution.py:606

commit v2 on v1

--- a/solution.py
+++ b/solution.py
@@ -344,10 +344,10 @@
         return found.astype(jnp.bfloat16) * relation, relation
 
     def coef_of(word, query):
-        times = nn_dot(times_ref[...], one_hot(times_ref.shape[1], packing.block(word)))
+        times = nn_dot(times_ref[...], one_hot(times_ref.shape[1], packing.block(word))).astype(jnp.bfloat16)
         bend = jnp.tanh(nn_dot(half_ref[...], query))
         below = (bend - 1.0).astype(jnp.bfloat16)
-        return (times * (bend + 1.0)).astype(jnp.bfloat16) + one_hot(share, packing.target(word), 0.5) * below
+        return times * (bend + 1.0).astype(jnp.bfloat16) + one_hot(share, packing.target(word), 0.5) * below
 
     def keep(coef, query, relation, new_query, new_relation):
         coef_ref[...] = coef
@@ -453,22 +453,16 @@
 def place_kernel(tables, unit, place_ref, *refs):
     pieces, (out_ref, sems) = refs[: len(tables)], refs[-2:]
     place = place_ref[0]
+    copies = []
     for k, (table, chosen) in enumerate(tables):
         row = pl.multiple_of(pick(table, place) * unit, 128)
-        copy = pltpu.make_async_copy(pieces[k], out_ref.at[pl.ds(row, pieces[k].shape[0]), :], sems.at[k])
-        if chosen is None:
-            copy.start()
-            continue
-
-        @pl.when(pick(chosen, place) == 1)
-        def _(copy=copy):
-            copy.start()
-            copy.wait()
-
-    for k, (table, chosen) in enumerate(tables):
-        if chosen is None:
-            row = pl.multiple_of(pick(table, place) * unit, 128)
-            pltpu.make_async_copy(pieces[k], out_ref.at[pl.ds(row, pieces[k].shape[0]), :], sems.at[k]).wait()
+        copies.append(pltpu.make_async_copy(pieces[k], out_ref.at[pl.ds(row, pieces[k].shape[0]), :], sems.at[k]))
+    for act in ("start", "wait"):
+        for copy, (_, chosen) in zip(copies, tables):
+            if chosen is None:
+                getattr(copy, act)()
+            else:
+                pl.when(pick(chosen, place) == 1)(getattr(copy, act))
 
 
 SMEM = pl.BlockSpec(memory_space=pltpu.SMEM)
@@ -530,8 +524,7 @@
             functools.partial(sort_kernel, packing, tiles, share), (place, *ids),
             (shape((reps * slots // TILE + 8, TILE), jnp.int32), shape((reps + 1,), jnp.int32),
              shape((8, 128), jnp.int32)),
-            [pltpu.VMEM((8, 128), jnp.int32), pltpu.SemaphoreType.DMA], "sort", 5, scalar_outs=(1, 2),
-            grant=40 * 1024 * 1024)
+            [pltpu.VMEM((8, 128), jnp.int32), pltpu.SemaphoreType.DMA], "sort", 5, scalar_outs=(1, 2))
 
     def gather_edges(place, codes, scales_row, *sent):
         ids = [sent[0]]

time: 84.5 us -> 84.2 us (level); the launches traced: 85.7 us -> 83.5 us
  starting transfers between devices: 17.8 us -> 29.2 us
  waiting for transfers between devices: 20.3 us -> 11.4 us
  Pallas kernels: 44.4 us -> 39.4 us
    ppermute x2, starting transfers between devices: 0.16 us -> 9.9 us  [branch(): lax.ppermute(block, 'dom', route(bits))]
    ppermute x2, waiting for transfers between devices: 10.2 us -> 5.2 us  [body(): far = [lax.ppermute(held, 'rep', across) for held in (low, high)]]
    pallas_call x11, Pallas kernels: 44.4 us -> 39.4 us  [call(): pl.pallas_call(kernel, out_shape=outs, in_specs=[SMEM] * scalars + [HBM]...]
    ppermute x2, waiting for transfers between devices: 2.11 us -> 0.28 us  [branch(): lax.ppermute(block, 'dom', route(bits))]
    ppermute x3, starting transfers between devices: 3.09 us -> 4.9 us  [body(): arrived = lax.ppermute(moving, 'rep', forward)]
    ppermute x3, waiting for transfers between devices: 2.42 us -> 1.02 us  [gather_edges(): ids.append(lax.ppermute(sent[apart], 'rep', along))]
  transfers between devices with their start and end apart: 14 -> 14, of which waited for: 9 -> 8; matrix products, arithmetic and copies ran while one was open for 0% -> 0% of each run, Pallas kernels for 36% -> 33%
where the time goes in v2:
time: 84.2 us; the launch traced here: 83.5 us
  Pallas kernels  39.4 us (47%)
  starting transfers between devices  29.2 us (35%)
  waiting for transfers between devices  11.4 us (14%)
  between operations  2.3 us (3%)
    pallas_call x11, Pallas kernels, call(): pl.pallas_call(kernel, out_shape=outs, in_specs=[SMEM] * scalars + [HBM]...  39.4 us
    ppermute x2, starting transfers between devices, branch(): lax.ppermute(block, 'dom', route(bits))  9.9 us
    ppermute x3, starting transfers between devices, gather_edges(): ids.append(lax.ppermute(sent[apart], 'rep', along))  7.01 us
    ppermute x2, waiting for transfers between devices, body(): far = [lax.ppermute(held, 'rep', across) for held in (low, high)]  5.2 us
    ppermute x3, starting transfers between devices, body(): arrived = lax.ppermute(moving, 'rep', forward)  4.9 us
    ppermute x2, waiting for transfers between devices, body(): ends = [lax.ppermute(held, 'rep', [(2, 3), (1, 0)]) for held in far]  4.63 us
    ppermute x2, starting transfers between devices, body(): far = [lax.ppermute(held, 'rep', across) for held in (low, high)]  2.92 us
    ppermute x2, starting transfers between devices, body(): ends = [lax.ppermute(held, 'rep', [(2, 3), (1, 0)]) for held in far]  2.56 us
  transfers between devices with their start and end apart: 14, of which 8 were waited for; matrix products, arithmetic and copies ran while one was open for 0% of the time, Pallas kernels for 33%

profile of v2, /device:TPU:0, one launch (start us, length us, event | category | flops | bytes accessed | tf_op | source)
XLA Modules:
  0.0 83.5 jit_solution(7304330984155920031)
XLA Ops:
  1.9 0.7 broadcast_in_dim.10.scales_hbm.scales_ref
  2.6 2.6 %open.1 = (s32[17,512]{1,0:T(8,128)S(1)}, s32[17,512]{1,0:T(8,128)S(1)}, s32[17,512]{1,0:T(8,128)S(1)}, s32[17,512]{1,0:T(8,128)S(1)}, bf16[256,512]{1,0:T(8,128...) custom-call(s32[1]{0:T(128)} %bitcast.place_ref, bf16[2048,256]{1,0:T(8,128)(2,1)} %codes_hbm.1, ...), custom_call_target="tpu_custom_call" | custom-call | flops 3449999872 | tf_op jit(solution)/shard_map/open/pallas_call | solution.py:477
  5.2 15.2 %conditional.2 = (bf16[256,512]{1,0:T(8,128)(2,1)}, bf16[256,2048]{1,0:T(8,128)(2,1)S(1)}, s32[17,512]{1,0:T(8,128)}, s32[17,512]{1,0:T(8,128)}, s32[17,512]{1,0...) conditional(s32[]{:T(128)} %clamp.4, ...), branch_computations={%region_0.1_spmd, %region_1.2_spmd, %region_2.3_spmd, %region_3.4_... | conditional | flops 8049999872 | bytes 1466592 | solution.py:32
  5.2 3.1 %collective-permute-start.5 = (s32[17,512]{1,0:T(8,128)S(1)}, s32[17,512]{1,0:T(8,128)}, u32[]{:S(2)}, u32[]{:S(2)}) collective-permute-start(s32[17,512]{1,0:T(8,128)S(1)} %get-tuple-element.238), channel_id=1, source_target_pairs={{0,1},{1,2},{2,3},{3,0},{4,5},{5,6},{6,7},{7,4},{8,9},{9,10},{10,1... | collective-permute-start | bytes 104456 | tf_op jit(solution)/shard_map/cond/branch_1_fun/ppermute | solution.py:533
  8.3 2.6 %collective-permute-start.6 = (s32[17,512]{1,0:T(8,128)S(1)}, s32[17,512]{1,0:T(8,128)}, u32[]{:S(2)}, u32[]{:S(2)}) collective-permute-start(s32[17,512]{1,0:T(8,128)S(1)} %get-tuple-element.239), channel_id=1, source_target_pairs={{0,2},{1,3},{2,0},{3,1},{4,6},{5,7},{6,4},{7,5},{8,10},{9,11},{10,... | collective-permute-start | bytes 104456 | tf_op jit(solution)/shard_map/cond/branch_1_fun/ppermute | solution.py:533
  10.9 1.3 %collective-permute-start.7 = (s32[17,512]{1,0:T(8,128)S(1)}, s32[17,512]{1,0:T(8,128)}, u32[]{:S(2)}, u32[]{:S(2)}) collective-permute-start(s32[17,512]{1,0:T(8,128)S(1)} %get-tuple-element.240), channel_id=1, source_target_pairs={{0,3},{1,0},{2,1},{3,2},{4,7},{5,4},{6,5},{7,6},{8,11},{9,8},{10,9... | collective-permute-start | bytes 104456 | tf_op jit(solution)/shard_map/cond/branch_1_fun/ppermute | solution.py:533
  12.3 1.5 %collective-permute-start.4 = (bf16[256,512]{1,0:T(8,128)(2,1)S(1)}, bf16[256,512]{1,0:T(8,128)(2,1)}, u32[]{:S(2)}, u32[]{:S(2)}) collective-permute-start(bf16[256,512]{1,0:T(8,128)(2,1)S(1)} %get-tuple-element.235), channel_id=1, source_target_pairs={{0,8},{4,12},{8,0},{12,4},{16,24},{20,28},{24,16},{28,20},{1,9},{5... | collective-permute-start | bytes 786440 | tf_op jit(solution)/shard_map/cond/branch_1_fun/ppermute | solution.py:30
  14.1 0.5 collective-permute-done.6.refs_2_
  14.6 0.5 collective-permute-done.7.refs_3_
  15.1 5.0 %sort.8 = (s32[40,512]{1,0:T(8,128)S(1)}, s32[5]{0:T(128)S(1)}, s32[8,128]{1,0:T(8,128)S(1)}) custom-call(s32[1]{0:T(128)} %get-tuple-element.241.place_ref, s32[17,512]{1,0:T(8,128)S(1)} %get-tuple-element.242.refs_0_, s32[17,512]{1,0:T(8,128)} %collective-permute-done.5.refs_1_, s32[17,512]{1,0:T(8,128)} %collective-permute-done.6.refs_2_, ...), custom_call_target="tpu_custom_call" | custom-call | flops 5750000128 | tf_op jit(solution)/shard_map/cond/branch_1_fun/jit(sort_edges)/sort/pallas_call | solution.py:477
  20.4 7.0 %part.4 = (bf16[512,256]{1,0:T(8,128)(2,1)S(1)}, f32[512,256]{1,0:T(8,128)S(1)}, bf16[512,512]{1,0:T(8,128)(2,1)S(1)}, bf16[256,512]{1,0:T(8,128)(2,1)S(1)}, bf1...) custom-call(s32[1]{0:T(128)} %bitcast.place_ref, ...), custom_call_target="tpu_custom_call" | custom-call | flops 10350000128 | tf_op jit(solution)/shard_map/part/pallas_call | solution.py:477
  27.3 1.1 %collective-permute-start.35 = (bf16[512,256]{1,0:T(8,128)(2,1)S(1)}, bf16[512,256]{1,0:T(8,128)(2,1)S(1)}, u32[]{:S(2)}, u32[]{:S(2)}) collective-permute-start(bf16[512,256]{1,0:T(8,128)(2,1)S(1)} %get-tuple-element.421), channel_id=1, source_target_pairs={{0,2},{2,3},{3,1},{1,0},{4,6},{6,7},{7,5},{5,4},{8,10},{10,11},{11... | collective-permute-start | bytes 786440 | tf_op jit(solution)/shard_map/ppermute | solution.py:573
  28.4 5.9 %part.5 = (bf16[512,256]{1,0:T(8,128)(2,1)S(1)}, f32[512,256]{1,0:T(8,128)S(1)}, bf16[512,512]{1,0:T(8,128)(2,1)S(1)}, bf16[256,512]{1,0:T(8,128)(2,1)S(1)}, bf1...) custom-call(s32[1]{0:T(128)} %bitcast.place_ref, ...), custom_call_target="tpu_custom_call", output_to_operand_aliasing={{1}: (9, {}), {2}: (10, {}), {3}: (11, {}), {4}: (12, {}), ... | custom-call | flops 10350000128 | tf_op jit(solution)/shard_map/part/pallas_call | solution.py:477
  34.7 2.4 %collective-permute-start.36 = (bf16[512,256]{1,0:T(8,128)(2,1)S(1)}, bf16[512,256]{1,0:T(8,128)(2,1)S(1)}, u32[]{:S(2)}, u32[]{:S(2)}) collective-permute-start(bf16[512,256]{1,0:T(8,128)(2,1)S(1)} %add_convert_fusion.1), channel_id=1, source_target_pairs={{0,2},{2,3},{3,1},{1,0},{4,6},{6,7},{7,5},{5,4},{8,10},{10,11},{11... | collective-permute-start | bytes 786440 | tf_op jit(solution)/shard_map/ppermute | solution.py:573
  37.1 5.9 %part.6 = (bf16[512,256]{1,0:T(8,128)(2,1)S(1)}, f32[512,256]{1,0:T(8,128)S(1)}, bf16[512,512]{1,0:T(8,128)(2,1)S(1)}, bf16[256,512]{1,0:T(8,128)(2,1)S(1)}, bf1...) custom-call(s32[1]{0:T(128)} %bitcast.place_ref, ...), custom_call_target="tpu_custom_call", output_to_operand_aliasing={{1}: (9, {}), {2}: (10, {}), {3}: (11, {}), {4}: (12, {}), ... | custom-call | flops 10350000128 | tf_op jit(solution)/shard_map/part/pallas_call | solution.py:477
  43.1 1.4 %collective-permute-start.37 = (bf16[512,256]{1,0:T(8,128)(2,1)S(1)}, bf16[512,256]{1,0:T(8,128)(2,1)S(1)}, u32[]{:S(2)}, u32[]{:S(2)}) collective-permute-start(bf16[512,256]{1,0:T(8,128)(2,1)S(1)} %add_convert_fusion), channel_id=1, source_target_pairs={{0,2},{2,3},{3,1},{1,0},{4,6},{6,7},{7,5},{5,4},{8,10},{10,11},{11... | collective-permute-start | bytes 786440 | tf_op jit(solution)/shard_map/ppermute | solution.py:575
  44.5 5.0 %part.7 = (f32[512,256]{1,0:T(8,128)S(1)}, bf16[512,256]{1,0:T(8,128)(2,1)S(1)}, bf16[10,512,512]{2,1,0:T(8,128)(2,1)S(1)}) custom-call(s32[1]{0:T(128)} %bitcast.place_ref, s32[5]{0:T(128)S(1)} %get-tuple-element.412.below_ref.refs_8_, s32[8,128]{1,0:T(8,128)S(1)} %get-tuple-element.413.ends_ref, s32[40,512]{1,0:T(8,128)S(1)} %get-tuple-element.414.keys_ref, ...), custom_call_target="tpu_custom_call" | custom-call | flops 10350000128 | tf_op jit(solution)/shard_map/part/pallas_call | solution.py:477
  49.6 12.9 %conditional.3 = (bf16[512,256]{1,0:T(8,128)(2,1)}, bf16[512,256]{1,0:T(8,128)(2,1)S(1)}) conditional(s32[]{:T(128)} %clamp.4, (bf16[512,256]{1,0:T(8,128)(2,1)S(1)}, s32[1]{0:T(128)}, s32[5]{0:T(128)S(1)}, s32[40,512]{1,0:T(8,128)S(1)}, f32[512,256]{1,0:T(8,128)S(1)}, /*index=5*/bf16[256,64]{1,0:T(8,128)(2,1)S(1)}, ...), branch_computations={%region_7.8_spmd, %region_8.9_spmd, %region_9.10_spmd, %region_10.... | conditional | flops 3449999872 | bytes 1048632 | solution.py:32
  49.6 8.4 %collective-permute-start.29 = (bf16[512,256]{1,0:T(8,128)(2,1)S(1)}, bf16[512,256]{1,0:T(8,128)(2,1)}, u32[]{:S(2)}, u32[]{:S(2)}) collective-permute-start(bf16[512,256]{1,0:T(8,128)(2,1)S(1)} %get-tuple-element.309), channel_id=1, source_target_pairs={{0,8},{4,12},{8,0},{12,4},{16,24},{20,28},{24,16},{28,20},{1,9},{5... | collective-permute-start | bytes 786440 | tf_op jit(solution)/shard_map/cond/branch_1_fun/ppermute | solution.py:30
  58.0 4.2 %finish.8 = bf16[512,256]{1,0:T(8,128)(2,1)S(1)} custom-call(s32[1]{0:T(128)} %get-tuple-element.310.place_ref, s32[5]{0:T(128)S(1)} %get-tuple-element.311.below_ref, s32[40,512]{1,0:T(8,128)S(1)} %get-tuple-element.312.keys_ref, f32[512,256]{1,0:T(8,128)S(1)} %get-tuple-element.313.src_grad_ref, bf16[256,64]{1,0:T(8,128)(2,1)S(1)} %get-tuple-element.314.rel_t_ref, ...), custom_call_target="tpu_custom_call" | custom-call | flops 3449999872 | tf_op jit(solution)/shard_map/cond/branch_1_fun/jit(finish)/finish/pallas_call | solution.py:477
  62.5 1.9 %update.1 = (bf16[512,256]{1,0:T(8,128)(2,1)S(1)}, bf16[256,256]{1,0:T(8,128)(2,1)S(1)}, bf16[256,256]{1,0:T(8,128)(2,1)S(1)}, f32[1,512]{1,0:T(1,128)}) custom-call(s32[1]{0:T(128)} %bitcast.place_ref, f32[256,512]{1,0:T(8,128)S(1)} %copy-done.1, bf16[1,2048]{1,0:T(2,128)(2,1)S(1)} %broadcast_in_dim.10.scales_hbm.scales_ref, f32[1,2048]{1,0:T(1,128)S(1)} %bitcast.5, ...), custom_call_target="tpu_custom_call" | custom-call | flops 2300000000 | tf_op jit(solution)/shard_map/update/pallas_call | solution.py:477
  64.4 1.2 %collective-permute-start.43 = (bf16[512,256]{1,0:T(8,128)(2,1)S(1)}, bf16[512,256]{1,0:T(8,128)(2,1)S(1)}, u32[]{:S(2)}, u32[]{:S(2)}) collective-permute-start(bf16[512,256]{1,0:T(8,128)(2,1)S(1)} %get-tuple-element.449.refs_0_), channel_id=1, source_target_pairs={{0,1},{1,0},{2,3},{3,2},{4,5},{5,4},{6,7},{7,6},{8,9},{9,8},{10,11... | collective-permute-start | bytes 786440 | tf_op jit(solution)/shard_map/ppermute | solution.py:597
  65.6 1.3 %collective-permute-start.39 = (bf16[256,256]{1,0:T(8,128)(2,1)S(1)}, bf16[256,256]{1,0:T(8,128)(2,1)S(1)}, u32[]{:S(2)}, u32[]{:S(2)}) collective-permute-start(bf16[256,256]{1,0:T(8,128)(2,1)S(1)} %get-tuple-element.450), channel_id=1, source_target_pairs={{0,2},{2,0},{1,3},{3,1},{4,6},{6,4},{5,7},{7,5},{8,10},{10,8},{9,1... | collective-permute-start | bytes 393224 | tf_op jit(solution)/shard_map/ppermute | solution.py:596
  66.9 1.6 %collective-permute-start.41 = (bf16[256,256]{1,0:T(8,128)(2,1)S(1)}, bf16[256,256]{1,0:T(8,128)(2,1)S(1)}, u32[]{:S(2)}, u32[]{:S(2)}) collective-permute-start(bf16[256,256]{1,0:T(8,128)(2,1)S(1)} %get-tuple-element.451), channel_id=1, source_target_pairs={{0,2},{2,0},{1,3},{3,1},{4,6},{6,4},{5,7},{7,5},{8,10},{10,8},{9,1... | collective-permute-start | bytes 393224 | tf_op jit(solution)/shard_map/ppermute | solution.py:596
  68.6 0.7 collective-permute-start.38
  69.2 5.1 %collective-permute-done.39.refs_2_ = bf16[256,256]{1,0:T(8,128)(2,1)S(1)} collective-permute-done((bf16[256,256]{1,0:T(8,128)(2,1)S(1)}, bf16[256,256]{1,0:T(8,128)(2,1)S(1)}, u32[]{:S(2)}, u32[]{:S(2)}) %collective-permute-start.39) | collective-permute-done | bytes 131104 | tf_op jit(solution)/shard_map/ppermute | solution.py:596
  74.3 1.3 %collective-permute-start.40 = (bf16[256,256]{1,0:T(8,128)(2,1)S(1)}, bf16[256,256]{1,0:T(8,128)(2,1)S(1)}, u32[]{:S(2)}, u32[]{:S(2)}) collective-permute-start(bf16[256,256]{1,0:T(8,128)(2,1)S(1)} %collective-permute-done.39.refs_2_), channel_id=1, source_target_pairs={{2,3},{1,0},{6,7},{5,4},{10,11},{9,8},{14,15},{13,12},{18,19},{17,... | collective-permute-start | bytes 393224 | tf_op jit(solution)/shard_map/ppermute | solution.py:599
  75.7 1.3 %collective-permute-start.42 = (bf16[256,256]{1,0:T(8,128)(2,1)S(1)}, bf16[256,256]{1,0:T(8,128)(2,1)S(1)}, u32[]{:S(2)}, u32[]{:S(2)}) collective-permute-start(bf16[256,256]{1,0:T(8,128)(2,1)S(1)} %collective-permute-done.41.refs_3_), channel_id=1, source_target_pairs={{2,3},{1,0},{6,7},{5,4},{10,11},{9,8},{14,15},{13,12},{18,19},{17,... | collective-permute-start | bytes 393224 | tf_op jit(solution)/shard_map/ppermute | solution.py:599
  77.0 0.9 %place.2.refs_3_ = bf16[2048,256]{1,0:T(8,128)(2,1)} custom-call(s32[1]{0:T(128)} %bitcast.place_ref, bf16[512,256]{1,0:T(8,128)(2,1)S(1)} %get-tuple-element.449.refs_0_, bf16[512,256]{1,0:T(8,128)(2,1)S(1)} %collective-permute-done.43.refs_1_, bf16[256,256]{1,0:T(8,128)(2,1)S(1)} %collective-permute-done.39.refs_2_, ...), custom_call_target="tpu_custom_call" | custom-call | flops 1150000000 | tf_op jit(solution)/shard_map/place/pallas_call | solution.py:477
  77.9 3.2 %collective-permute-done.40.refs_1_ = bf16[256,256]{1,0:T(8,128)(2,1)S(1)} collective-permute-done((bf16[256,256]{1,0:T(8,128)(2,1)S(1)}, bf16[256,256]{1,0:T(8,128)(2,1)S(1)}, u32[]{:S(2)}, u32[]{:S(2)}) %collective-permute-start.40) | collective-permute-done | bytes 131104 | tf_op jit(solution)/shard_map/ppermute | solution.py:599
  81.2 1.4 %collective-permute-done.42.refs_2_ = bf16[256,256]{1,0:T(8,128)(2,1)S(1)} collective-permute-done((bf16[256,256]{1,0:T(8,128)(2,1)S(1)}, bf16[256,256]{1,0:T(8,128)(2,1)S(1)}, u32[]{:S(2)}, u32[]{:S(2)}) %collective-permute-start.42) | collective-permute-done | bytes 131104 | tf_op jit(solution)/shard_map/ppermute | solution.py:599
  82.6 0.7 place.3
  (18 shorter events, 1.2 us)
Async XLA Ops:
  2.6 2.6 %copy-start.2 = (bf16[2048,256]{1,0:T(8,128)(2,1)S(1)}, bf16[2048,256]{1,0:T(8,128)(2,1)}, u32[]{:S(2)}) copy-start(bf16[2048,256]{1,0:T(8,128)(2,1)} %codes_hbm.1) | copy-start | bytes 3145732
  5.2 8.9 %collective-permute-start.5 = (s32[17,512]{1,0:T(8,128)S(1)}, s32[17,512]{1,0:T(8,128)}, u32[]{:S(2)}, u32[]{:S(2)}) collective-permute-start(s32[17,512]{1,0:T(8,128)S(1)} %get-tuple-element.238), channel_id=1, source_target_pairs={{0,1},{1,2},{2,3},{3,0},{4,5},{5,6},{6,7},{7,4},{8,9},{9,10},{10,1... | collective-permute-start | bytes 104456 | tf_op jit(solution)/shard_map/cond/branch_1_fun/ppermute | solution.py:533
  8.3 6.3 %collective-permute-start.6 = (s32[17,512]{1,0:T(8,128)S(1)}, s32[17,512]{1,0:T(8,128)}, u32[]{:S(2)}, u32[]{:S(2)}) collective-permute-start(s32[17,512]{1,0:T(8,128)S(1)} %get-tuple-element.239), channel_id=1, source_target_pairs={{0,2},{1,3},{2,0},{3,1},{4,6},{5,7},{6,4},{7,5},{8,10},{9,11},{10,... | collective-permute-start | bytes 104456 | tf_op jit(solution)/shard_map/cond/branch_1_fun/ppermute | solution.py:533
  10.9 4.2 %collective-permute-start.7 = (s32[17,512]{1,0:T(8,128)S(1)}, s32[17,512]{1,0:T(8,128)}, u32[]{:S(2)}, u32[]{:S(2)}) collective-permute-start(s32[17,512]{1,0:T(8,128)S(1)} %get-tuple-element.240), channel_id=1, source_target_pairs={{0,3},{1,0},{2,1},{3,2},{4,7},{5,4},{6,5},{7,6},{8,11},{9,8},{10,9... | collective-permute-start | bytes 104456 | tf_op jit(solution)/shard_map/cond/branch_1_fun/ppermute | solution.py:533
  12.3 7.9 %collective-permute-start.4 = (bf16[256,512]{1,0:T(8,128)(2,1)S(1)}, bf16[256,512]{1,0:T(8,128)(2,1)}, u32[]{:S(2)}, u32[]{:S(2)}) collective-permute-start(bf16[256,512]{1,0:T(8,128)(2,1)S(1)} %get-tuple-element.235), channel_id=1, source_target_pairs={{0,8},{4,12},{8,0},{12,4},{16,24},{20,28},{24,16},{28,20},{1,9},{5... | collective-permute-start | bytes 786440 | tf_op jit(solution)/shard_map/cond/branch_1_fun/ppermute | solution.py:30
  27.3 7.3 %collective-permute-start.35 = (bf16[512,256]{1,0:T(8,128)(2,1)S(1)}, bf16[512,256]{1,0:T(8,128)(2,1)S(1)}, u32[]{:S(2)}, u32[]{:S(2)}) collective-permute-start(bf16[512,256]{1,0:T(8,128)(2,1)S(1)} %get-tuple-element.421), channel_id=1, source_target_pairs={{0,2},{2,3},{3,1},{1,0},{4,6},{6,7},{7,5},{5,4},{8,10},{10,11},{11... | collective-permute-start | bytes 786440 | tf_op jit(solution)/shard_map/ppermute | solution.py:573
  34.7 8.3 %collective-permute-start.36 = (bf16[512,256]{1,0:T(8,128)(2,1)S(1)}, bf16[512,256]{1,0:T(8,128)(2,1)S(1)}, u32[]{:S(2)}, u32[]{:S(2)}) collective-permute-start(bf16[512,256]{1,0:T(8,128)(2,1)S(1)} %add_convert_fusion.1), channel_id=1, source_target_pairs={{0,2},{2,3},{3,1},{1,0},{4,6},{6,7},{7,5},{5,4},{8,10},{10,11},{11... | collective-permute-start | bytes 786440 | tf_op jit(solution)/shard_map/ppermute | solution.py:573
  43.1 19.3 %collective-permute-start.37 = (bf16[512,256]{1,0:T(8,128)(2,1)S(1)}, bf16[512,256]{1,0:T(8,128)(2,1)S(1)}, u32[]{:S(2)}, u32[]{:S(2)}) collective-permute-start(bf16[512,256]{1,0:T(8,128)(2,1)S(1)} %add_convert_fusion), channel_id=1, source_target_pairs={{0,2},{2,3},{3,1},{1,0},{4,6},{6,7},{7,5},{5,4},{8,10},{10,11},{11... | collective-permute-start | bytes 786440 | tf_op jit(solution)/shard_map/ppermute | solution.py:575
  49.5 12.9 %copy-start = (f32[2048]{0:T(1024)S(1)}, f32[2048]{0:T(1024)}, u32[]{:S(2)}) copy-start(f32[2048]{0:T(1024)} %param.24) | copy-start | bytes 24580
  49.5 12.9 %copy-start.1 = (f32[256,512]{1,0:T(8,128)S(1)}, f32[256,512]{1,0:T(8,128)}, u32[]{:S(2)}) copy-start(f32[256,512]{1,0:T(8,128)} %get-tuple-element.406.values_t_ref) | copy-start | bytes 1572868
  49.6 12.9 %collective-permute-start.29 = (bf16[512,256]{1,0:T(8,128)(2,1)S(1)}, bf16[512,256]{1,0:T(8,128)(2,1)}, u32[]{:S(2)}, u32[]{:S(2)}) collective-permute-start(bf16[512,256]{1,0:T(8,128)(2,1)S(1)} %get-tuple-element.309), channel_id=1, source_target_pairs={{0,8},{4,12},{8,0},{12,4},{16,24},{20,28},{24,16},{28,20},{1,9},{5... | collective-permute-start | bytes 786440 | tf_op jit(solution)/shard_map/cond/branch_1_fun/ppermute | solution.py:30
  64.4 12.6 %collective-permute-start.43 = (bf16[512,256]{1,0:T(8,128)(2,1)S(1)}, bf16[512,256]{1,0:T(8,128)(2,1)S(1)}, u32[]{:S(2)}, u32[]{:S(2)}) collective-permute-start(bf16[512,256]{1,0:T(8,128)(2,1)S(1)} %get-tuple-element.449.refs_0_), channel_id=1, source_target_pairs={{0,1},{1,0},{2,3},{3,2},{4,5},{5,4},{6,7},{7,6},{8,9},{9,8},{10,11... | collective-permute-start | bytes 786440 | tf_op jit(solution)/shard_map/ppermute | solution.py:597
  65.6 8.7 %collective-permute-start.39 = (bf16[256,256]{1,0:T(8,128)(2,1)S(1)}, bf16[256,256]{1,0:T(8,128)(2,1)S(1)}, u32[]{:S(2)}, u32[]{:S(2)}) collective-permute-start(bf16[256,256]{1,0:T(8,128)(2,1)S(1)} %get-tuple-element.450), channel_id=1, source_target_pairs={{0,2},{2,0},{1,3},{3,1},{4,6},{6,4},{5,7},{7,5},{8,10},{10,8},{9,1... | collective-permute-start | bytes 393224 | tf_op jit(solution)/shard_map/ppermute | solution.py:596
  66.9 8.8 %collective-permute-start.41 = (bf16[256,256]{1,0:T(8,128)(2,1)S(1)}, bf16[256,256]{1,0:T(8,128)(2,1)S(1)}, u32[]{:S(2)}, u32[]{:S(2)}) collective-permute-start(bf16[256,256]{1,0:T(8,128)(2,1)S(1)} %get-tuple-element.451), channel_id=1, source_target_pairs={{0,2},{2,0},{1,3},{3,1},{4,6},{6,4},{5,7},{7,5},{8,10},{10,8},{9,1... | collective-permute-start | bytes 393224 | tf_op jit(solution)/shard_map/ppermute | solution.py:596
  68.6 14.0 %collective-permute-start.38 = (bf16[512,256]{1,0:T(8,128)(2,1)S(1)}, bf16[512,256]{1,0:T(8,128)(2,1)S(1)}, u32[]{:S(2)}, u32[]{:S(2)}) collective-permute-start(bf16[512,256]{1,0:T(8,128)(2,1)S(1)} %get-tuple-element.449.refs_0_), channel_id=1, source_target_pairs={{1,2},{2,1},{5,6},{6,5},{9,10},{10,9},{13,14},{14,13},{17,18},{18,... | collective-permute-start | bytes 786440 | tf_op jit(solution)/shard_map/ppermute | solution.py:598
  74.3 6.8 %collective-permute-start.40 = (bf16[256,256]{1,0:T(8,128)(2,1)S(1)}, bf16[256,256]{1,0:T(8,128)(2,1)S(1)}, u32[]{:S(2)}, u32[]{:S(2)}) collective-permute-start(bf16[256,256]{1,0:T(8,128)(2,1)S(1)} %collective-permute-done.39.refs_2_), channel_id=1, source_target_pairs={{2,3},{1,0},{6,7},{5,4},{10,11},{9,8},{14,15},{13,12},{18,19},{17,... | collective-permute-start | bytes 393224 | tf_op jit(solution)/shard_map/ppermute | solution.py:599
  75.7 6.8 %collective-permute-start.42 = (bf16[256,256]{1,0:T(8,128)(2,1)S(1)}, bf16[256,256]{1,0:T(8,128)(2,1)S(1)}, u32[]{:S(2)}, u32[]{:S(2)}) collective-permute-start(bf16[256,256]{1,0:T(8,128)(2,1)S(1)} %collective-permute-done.41.refs_3_), channel_id=1, source_target_pairs={{2,3},{1,0},{6,7},{5,4},{10,11},{9,8},{14,15},{13,12},{18,19},{17,... | collective-permute-start | bytes 393224 | tf_op jit(solution)/shard_map/ppermute | solution.py:599
